TPU v7x, 512 devices: a whole 4x8x8 slice. The times are simulated.
512 devices in a mesh: tile: 64 (over y, z_hi, x), lev: 8 (over z_lo, core).
Axes of the slice: x: 4, y: 8, z: 8 (z_hi: 2, z_lo: 4; z = z_hi * 4 + z_lo), core: 2. Of those that a mesh axis runs over, the one named last changes fastest.
Arguments:
- adjoint: float32 [4, 32, 2048, 256], P(None, 'lev', 'tile'), may hold values from -6 to 6
- wind_x: float32 [32, 2048, 256], P('lev', 'tile'), may hold values from -0.25 to 0.25
- wind_y: float32 [32, 2048, 256], P('lev', 'tile'), may hold values from -0.25 to 0.25
- kz: float32 [32, 2048, 256], P('lev', 'tile'), may hold values from 10 to 400
- forcing: float32 [64, 64, 4, 32, 32], P('tile', None, None, 'lev'), may hold values from -6 to 6
- mon_cols: int32 [64, 64, 32], P('tile'), may hold values from 0 to 8191
- mon_counts: int32 [64, 64], P('tile'), may hold values from 0 to 32, as said below
Outputs:
- updated: float32 [4, 32, 2048, 256], P(None, 'lev', 'tile')
Inputs may be any that keep to these rules, and one draw needn't show every extreme that they name: `mon_counts`: in every draw one owning strip has all 32 slots used from every sending strip.
All inputs are finite; a program needn't handle non-finite values.
Results may differ from a plain program's by a relative error of at most 0.00016.
Values sent between devices are 32-bit elements; how exact they have to be, the bound alone decides.
No kernel may reach another device: no remote copies, remote signals or barrier semaphores. Data moves between devices by JAX's collectives and lax.ppermute only.
A program may use at most 128 MiB of HBM per device.

v0:
```python
import jax
import jax.numpy as jnp
from jax import lax
from jax.sharding import PartitionSpec as P


def extended(shard, sides, width):
    for axis, dim in sides:
        size, length = (lax.axis_size(axis), shard.shape[dim])
        up = [(i, (i + 1) % size) for i in range(size)]
        down = [(j, i) for i, j in up]
        last = lax.slice_in_dim(shard, length - width, length, axis=dim)
        initial = lax.slice_in_dim(shard, 0, width, axis=dim)
        before = lax.ppermute(last, axis, up)
        after = lax.ppermute(initial, axis, down)
        shard = jnp.concatenate([before, shard, after], axis=dim)
    return shard


def tri_solve(lower_band, main_band, upper_band, right_side):
    count_levels = right_side.shape[1]
    ratios = []
    scaled = []
    for level_id in range(count_levels):
        if level_id == 0:
            pivot_value = main_band[0]
            scaled.append(right_side[:, 0] / pivot_value)
        else:
            pivot_value = main_band[level_id] - lower_band[level_id] * ratios[level_id - 1]
            scaled.append(
                (right_side[:, level_id] - lower_band[level_id] * scaled[level_id - 1])
                / pivot_value
            )
        ratios.append(upper_band[level_id] / pivot_value)
    solution = [scaled[-1]]
    for level_id in range(count_levels - 2, -1, -1):
        solution.append(scaled[level_id] - ratios[level_id] * solution[-1])
    return jnp.stack(solution[::-1], 1)


def column_system(coupling, coupling_first):
    coupling_below = jnp.concatenate([coupling_first[None], coupling[:-1]], 0)
    return (-coupling_below, 1.0 + coupling_below + coupling, -coupling)


def transport(field, wind_east, wind_west, wind_y, east_side, west_side):
    lat_count = field.shape[-1]
    latitude = lax.broadcasted_iota(jnp.int32, wind_y.shape, wind_y.ndim - 1)
    wind_north = jnp.where(latitude == lat_count - 1, 0.0, wind_y)
    wind_south = jnp.pad(wind_north, [(0, 0)] * (wind_y.ndim - 1) + [(1, 0)])[..., :-1]
    north_side = jnp.pad(field, [(0, 0)] * (field.ndim - 1) + [(0, 1)])[..., 1:]
    south_side = jnp.pad(field, [(0, 0)] * (field.ndim - 1) + [(1, 0)])[..., :-1]
    return (
        field
        + jnp.maximum(wind_east, 0.0) * (east_side - field)
        - jnp.minimum(wind_west, 0.0) * (west_side - field)
        + jnp.maximum(wind_north, 0.0) * (north_side - field)
        - jnp.minimum(wind_south, 0.0) * (south_side - field)
    )


def inject_rows(field, forcing_rows, column_ids):
    tracer_count, lev_dev = (field.shape[0], field.shape[1])
    is_valid = column_ids >= 0
    flat_index = jnp.where(is_valid, column_ids, 0).reshape(-1)
    masked_rows = jnp.where(is_valid[:, None, None, :], forcing_rows, 0.0)
    masked_rows = jnp.transpose(masked_rows, (1, 2, 0, 3)).reshape(tracer_count, lev_dev, -1)
    flat_field = field.reshape(tracer_count, lev_dev, -1)
    return flat_field.at[:, :, flat_index].add(masked_rows).reshape(field.shape)


def settle(column_block):
    tracer_count = column_block.shape[0] - 1
    levels_all = column_block.shape[1]
    level_id = lax.broadcasted_iota(jnp.int32, column_block.shape[1:], 0)
    coupling = jnp.where(level_id == levels_all - 1, 0.0, column_block[tracer_count])
    lower_band, main_band, upper_band = column_system(coupling, jnp.zeros_like(coupling[0]))
    solved = tri_solve(lower_band, main_band, upper_band, column_block[:tracer_count])
    return lax.all_to_all(solved, "lev", split_axis=1, concat_axis=2, tiled=True)


def per_device(adjoint, wind_x, wind_y, kz, forcing, mon_cols, mon_counts):
    tracer_count = adjoint.shape[0]
    stacked = jnp.concatenate([adjoint, wind_x[None]], 0)
    padded = extended(stacked, (("tile", 2),), 1)
    east_side = padded[:tracer_count, :, 2:]
    west_side = padded[:tracer_count, :, :-2]
    wind_west = padded[tracer_count, :, :-2]
    advected = transport(adjoint, wind_x, wind_west, wind_y, east_side, west_side)
    slot_id = lax.broadcasted_iota(jnp.int32, mon_cols.shape, 2)
    masked_cols = jnp.where(slot_id < mon_counts[:, :, None], mon_cols, -1)
    tile_index = lax.axis_index("tile")
    row_piece = lax.all_gather(forcing, "tile", axis=0, tiled=True)
    column_piece = lax.all_gather(masked_cols, "tile", axis=0, tiled=True)
    own_rows = lax.dynamic_index_in_dim(row_piece, tile_index, 1, keepdims=False)
    own_cols = lax.dynamic_index_in_dim(column_piece, tile_index, 1, keepdims=False)
    forced = inject_rows(advected, own_rows, own_cols)
    column_input = jnp.concatenate([forced, kz[None]], 0)
    updated = settle(lax.all_to_all(column_input, "lev", split_axis=2, concat_axis=1, tiled=True))
    return updated


def solution(mesh):
    in_specs = (
        P(None, "lev", "tile", None),
        P("lev", "tile", None),
        P("lev", "tile", None),
        P("lev", "tile", None),
        P("tile", None, None, "lev", None),
        P("tile", None, None),
        P("tile", None),
    )
    out_specs = P(None, "lev", "tile", None)
    return jax.shard_map(
        per_device, mesh=mesh, in_specs=in_specs, out_specs=out_specs, check_vma=False
    )
```

profile of v0, /device:TPU:6, one launch (start us, length us, event | category | flops | bytes accessed | tf_op | source)
XLA Modules:
  0.0 651.0 jit_solution(13546338696045082239)
XLA Ops:
  6.5 0.0 all-gather.2.cloned.1.call-start
  6.5 0.7 all-gather.2.cloned.1.call-update
  7.3 1.0 pad_maximum_fusion.6
  8.3 2.7 collective-permute-start
  11.0 10.0 %collective-permute-start.1 = (f32[5,4,1,256]{3,2,1,0:T(1,128)S(1)}, f32[5,4,1,256]{3,2,1,0:T(1,128)S(1)}, u32[]{:S(2)}, u32[]{:S(2)}) collective-permute-start(f32[5,4,1,256]{3,2,1,0:T(1,128)S(1)} %get-tuple-element.76), channel_id=1, source_target_pairs={{0,8},{8,16},{16,24},{24,32},{32,40},{40,48},{48,56},{56,64},{64,7... | collective-permute-start | bytes 61448 | tf_op jit(solution)/shard_map/ppermute | solution.py:14
  21.1 0.7 fusion.46
  21.8 222.6 %all_gather.6 = s32[64,64,32]{1,2,0:T(8,128)S(1)} all-gather(s32[1,64,32]{1,2,0:T(8,128)S(1)} %fusion.46), channel_id=1, replica_groups=mesh['tile'=64,'lev'=8] {'tile'}, dimensions={0}, use_global_device_ids=true | all-gather | bytes 532480 | tf_op jit(solution)/shard_map/all_gather | solution.py:94
  244.4 1.4 fusion.124
  245.8 0.1 squeeze.10
  245.9 0.6 copy.43
  246.5 0.9 broadcast_maximum_fusion
  247.5 1.0 fusion.13
  248.5 1.0 copy.47
  249.5 0.0 collective-permute-done.1
  249.5 0.9 fusion.14
  250.5 0.0 collective-permute-done
  250.5 2.7 fusion.3
  253.2 8.6 %copy.27 = f32[4,4,32,256]{1,0,3,2:T(4,128)} copy(f32[4,4,32,256]{3,2,1,0:T(8,128)S(1)} %fusion.3) | data formatting | bytes 1048576 | tf_op jit(solution)/shard_map/sub | solution.py:54
  261.8 65.0 %all-gather.2.cloned.1.call-done = f32[64,64,4,4,32]{1,4,3,2,0:T(8,128)} async-done(((f32[1,64,4,4,32]{1,4,3,2,0:T(8,128)}), f32[64,64,4,4,32]{1,4,3,2,0:T(8,128)}) %all-gather.2.cloned.1.call-update) | async-done | bytes 8388624 | tf_op jit(solution)/shard_map/all_gather | solution.py:93
  326.8 12.7 %constant_dynamic-slice_fusion = f32[64,1,4,4,32]{1,4,3,2,0:T(8,128)} fusion(f32[64,64,4,4,32]{1,4,3,2,0:T(8,128)} %all-gather.2.cloned.1.call-done, s32[]{:T(128)S(6)} %select_n.46), kind=kLoop, calls=%fused_computation.291 | loop fusion | bytes 262148 | tf_op jit(solution)/shard_map/jit(dynamic_index_in_dim)/dynamic_slice | solution.py:95
  339.6 11.9 %copy.44 = f32[64,1,4,4,32]{0,4,3,2,1:T(8,128)S(1)} copy(f32[64,1,4,4,32]{1,4,3,2,0:T(8,128)} %constant_dynamic-slice_fusion) | data formatting | bytes 262144
  351.5 0.2 copy.31
  351.7 0.3 reshape.91
  352.0 3.1 copy.32
  355.1 232.6 %scatter_fusion = f32[4,4,8192]{1,0,2:T(4,128)} fusion(f32[4,4,8192]{1,0,2:T(4,128)} %bitcast.188, s32[2048]{0:T(1024)S(1)} %bitcast.251, f32[2048,4,4]{2,1,0:T(4,128)} %copy.32), kind=kCustom, calls=%fused_computation | custom fusion | flops 32768 | bytes 401408 | tf_op jit(solution)/shard_map/scatter-add | solution.py:69
  587.7 12.9 %copy.34 = f32[4,4,32,256]{3,1,0,2:T(4,128)S(1)} copy(f32[4,4,32,256]{1,0,3,2:T(4,128)} %bitcast.189) | data formatting | bytes 1048576 | tf_op jit(solution)/shard_map/reshape | solution.py:69
  600.6 1.0 pad_maximum_fusion
  601.6 3.5 all-to-all-start
  605.2 18.1 %all-to-all-done = f32[5,4,32,256]{3,1,0,2:T(4,128)S(1)} async-done(((f32[5,4,32,256]{3,1,0,2:T(4,128)}), f32[5,4,32,256]{3,1,0,2:T(4,128)S(1)}, u32[]{:S(2)}, u32[]{:S(2)}) %all-to-all-start) | async-done | bytes 655392 | tf_op jit(solution)/shard_map/all_to_all | solution.py:99
  623.2 0.1 copy.35
  623.5 0.1 fusion.123
  623.7 0.1 copy.36
  623.9 0.3 fusion.47
  624.3 0.3 constant_dynamic-update-slice_fusion.31
  625.1 0.1 copy.38
  625.2 17.8 %all_to_all.33 = f32[4,32,4,256]{3,2,0,1:T(4,128)S(1)} all-to-all(f32[4,32,4,256]{3,2,0,1:T(4,128)S(1)} %copy.38), channel_id=1, replica_groups=mesh['tile'=64,'lev'=8] {'lev'}, dimensions={1} | all-to-all | bytes 1048576 | tf_op jit(solution)/shard_map/all_to_all | solution.py:79
  642.9 0.3 copy.40
  643.3 0.9 copy.41
  (48 shorter events, 0.7 us)
Async XLA Ops:
  6.5 320.3 %all-gather.2.cloned.1.call-start = ((), (), s32[]{:S(2)}) async-start(), calls=%async_computation.2 | async-start | bytes 17039360 | tf_op jit(solution)/shard_map/all_gather | solution.py:93
  8.3 242.2 %collective-permute-start = (f32[5,4,1,256]{3,2,1,0:T(1,128)S(1)}, f32[5,4,1,256]{3,2,1,0:T(1,128)S(1)}, u32[]{:S(2)}, u32[]{:S(2)}) collective-permute-start(f32[5,4,1,256]{3,2,1,0:T(1,128)S(1)} %get-tuple-element.75), channel_id=1, source_target_pairs={{8,0},{16,8},{24,16},{32,24},{40,32},{48,40},{56,48},{64,56},{72,6... | collective-permute-start | bytes 61448 | tf_op jit(solution)/shard_map/ppermute | solution.py:15
  11.0 238.5 %collective-permute-start.1 = (f32[5,4,1,256]{3,2,1,0:T(1,128)S(1)}, f32[5,4,1,256]{3,2,1,0:T(1,128)S(1)}, u32[]{:S(2)}, u32[]{:S(2)}) collective-permute-start(f32[5,4,1,256]{3,2,1,0:T(1,128)S(1)} %get-tuple-element.76), channel_id=1, source_target_pairs={{0,8},{8,16},{16,24},{24,32},{32,40},{40,48},{48,56},{56,64},{64,7... | collective-permute-start | bytes 61448 | tf_op jit(solution)/shard_map/ppermute | solution.py:14
  601.6 21.6 %all-to-all-start = ((f32[5,4,32,256]{3,1,0,2:T(4,128)}), f32[5,4,32,256]{3,1,0,2:T(4,128)S(1)}, u32[]{:S(2)}, u32[]{:S(2)}) async-start(f32[5,4,32,256]{3,1,0,2:T(4,128)} %pad_maximum_fusion), calls=%async_computation | async-start | bytes 1310720 | tf_op jit(solution)/shard_map/all_to_all | solution.py:99
Sparse Core Ops, SparseCore 0:
  11.7 315.0 all-gather.1
where the time goes:
time: 664 us; the launch traced here: 651 us
  other arithmetic  242 us (36%)
  blocking collectives  240 us (36%)
  waiting for transfers between devices  83.8 us (13%)
  local copies, waits for them, and re-layouts  54.7 us (8%)
  starting transfers between devices  16.3 us (2%)
  between operations  13.7 us (2%)
    scatter-add x1, other arithmetic, inject_rows(): return flat_field.at[:, :, flat_index].add(masked_rows).reshape(field.shape)  233 us
    all_gather x1, blocking collectives, per_device(): column_piece = lax.all_gather(masked_cols, 'tile', axis=0, tiled=True)  223 us
    all_gather x1, waiting for transfers between devices, per_device(): row_piece = lax.all_gather(forcing, 'tile', axis=0, tiled=True)  65 us
    all_to_all x1, waiting for transfers between devices, per_device(): lax.all_to_all(column_input, 'lev', split_axis=2, concat_axis=1, tiled=True)  18.1 us
    all_to_all x1, blocking collectives, settle(): lax.all_to_all(solved, 'lev', split_axis=1, concat_axis=2, tiled=True)  17.8 us
    unnamed x18, local copies, waits for them, and re-layouts  13.7 us
  transfers between devices with their start and end apart: 4, of which 2 were waited for; matrix products, arithmetic and copies ran while one was open for 3% of the time, Pallas kernels for 0%

commit v1 on v0

v1 whole, which is shorter than its diff:
```python
import jax
import jax.numpy as jnp
from jax import lax
from jax.experimental import pallas as pl
from jax.experimental.pallas import tpu as pltpu
from jax.sharding import PartitionSpec as P

TRACERS = 4
LEV_DEV = 4
NLEV = 32
LON = 32
LAT = 256
TILES = 64
CAP = 32
HALF = LON // 2
ROWS = TRACERS * LEV_DEV
VMEM = pl.BlockSpec(memory_space=pltpu.VMEM)
SMEM = pl.BlockSpec(memory_space=pltpu.SMEM)
F32 = jnp.float32


def call(body, outs, in_specs, scratch=(), limit=12 << 20, flops=0, moved=1 << 20, **more):
    shapes = tuple(jax.ShapeDtypeStruct(shape, F32) for shape in outs)
    return pl.pallas_call(
        body,
        out_shape=shapes,
        in_specs=in_specs,
        out_specs=tuple(VMEM for _ in outs),
        scratch_shapes=list(scratch),
        compiler_params=pltpu.CompilerParams(vmem_limit_bytes=limit),
        cost_estimate=pl.CostEstimate(flops=flops, bytes_accessed=moved, transcendentals=0),
        **more,
    )


def pack_body(force, cols, counts, low_adj, high_adj, high_wind, payload, low, high):
    slot = lax.broadcasted_iota(jnp.int32, (CAP, TILES), 0)
    valid = slot < counts[...]
    lon = jnp.where(valid, cols[...] >> 8, -1).astype(F32)
    lat = (cols[...] & 255).astype(F32)
    rest = jnp.zeros((56, TILES), F32)
    for i in range(8):
        parts = [force[pl.ds(4 * i + g, ROWS, stride=CAP), :] for g in range(4)]
        block = jnp.concatenate(parts + [lon[4 * i : 4 * i + 4], lat[4 * i : 4 * i + 4], rest], 0)
        payload[:, i, :] = block.T
    low[...] = low_adj[:, 0, :]
    high[0:ROWS, :] = high_adj[:, 7, :]
    high[ROWS : ROWS + LEV_DEV, :] = high_wind[:, 7, :]


def pack(forcing, mon_cols, mon_counts, adjoint, wind_x):
    force = jnp.transpose(forcing[0], (1, 2, 3, 0)).reshape(ROWS * CAP, TILES)
    cols = jnp.transpose(mon_cols[0], (1, 0))
    specs = [
        VMEM,
        VMEM,
        VMEM,
        pl.BlockSpec((ROWS, 8, LAT), lambda i: (0, 0, 0)),
        pl.BlockSpec((ROWS, 8, LAT), lambda i: (0, 3, 0)),
        pl.BlockSpec((LEV_DEV, 8, LAT), lambda i: (0, 3, 0)),
    ]
    outs = ((TILES, 8, 128), (ROWS, LAT), (ROWS + LEV_DEV, LAT))
    return call(pack_body, outs, specs, grid=(1,))(force, cols, mon_counts, adjoint, adjoint, wind_x)


def advect_body(adj, wind_x, wind_y, west, east, out):
    row = lax.broadcasted_iota(jnp.int32, (LON, LAT), 0)
    lane = lax.broadcasted_iota(jnp.int32, (LON, LAT), 1)
    for lev in range(LEV_DEV):
        cx = wind_x[lev]
        cx_west = jnp.where(row == 0, west[ROWS + lev : ROWS + lev + 1, :], pltpu.roll(cx, 1, 0))
        cy_n = jnp.where(lane == LAT - 1, 0.0, wind_y[lev])
        cy_s = pltpu.roll(cy_n, 1, 1)
        to_east = jnp.maximum(cx, 0.0)
        to_west = jnp.minimum(cx_west, 0.0)
        to_north = jnp.maximum(cy_n, 0.0)
        to_south = jnp.minimum(cy_s, 0.0)
        for tracer in range(TRACERS):
            n = tracer * LEV_DEV + lev
            a = adj[n]
            a_east = jnp.where(row == LON - 1, east[n : n + 1, :], pltpu.roll(a, LON - 1, 0))
            a_west = jnp.where(row == 0, west[n : n + 1, :], pltpu.roll(a, 1, 0))
            a_north = pltpu.roll(a, LAT - 1, 1)
            a_south = pltpu.roll(a, 1, 1)
            out[n] = (
                a
                + to_east * (a_east - a)
                - to_west * (a_west - a)
                + to_north * (a_north - a)
                - to_south * (a_south - a)
            )


def weights_body(place, kz, up, down, inverse, chip_up, chip_down, core_up, core_down, up_all, down_all, low, high):
    lev = place[0]
    core = lev % 2
    below = jnp.zeros((LON, LAT), F32)
    for l in range(NLEV):
        low[l] = below
        if l < NLEV - 1:
            k = kz[l]
            ground = 1.0 + below
            up_all[l] = k / (ground + k)
            below = up_all[l] * ground
        else:
            up_all[l] = jnp.zeros((LON, LAT), F32)
    above = jnp.zeros((LON, LAT), F32)
    for l in range(NLEV - 1, -1, -1):
        high[l] = above
        if l > 0:
            k = kz[l - 1]
            ground = 1.0 + above
            down_all[l] = k / (ground + k)
            above = down_all[l] * ground
        else:
            down_all[l] = jnp.zeros((LON, LAT), F32)
    mine = pl.ds(lev * LEV_DEV, LEV_DEV)
    up[...] = up_all[mine]
    down[...] = down_all[mine]
    inverse[...] = 1.0 / (1.0 + low[mine] + high[mine])
    half = pl.ds(pl.multiple_of(core * HALF, HALF), HALF)
    for chip in range(4):
        ups = [up_all[8 * chip + n, half, :] for n in range(8)]
        downs = [down_all[8 * chip + n, half, :] for n in range(8)]
        up_low, up_high = (ups[0] * ups[1]) * (ups[2] * ups[3]), (ups[4] * ups[5]) * (ups[6] * ups[7])
        down_low, down_high = (downs[0] * downs[1]) * (downs[2] * downs[3]), (downs[4] * downs[5]) * (downs[6] * downs[7])
        chip_up[chip] = up_low * up_high
        chip_down[chip] = down_low * down_high

        @pl.when(lev // 2 == chip)
        def _():
            core_up[0] = up_low
            core_up[1] = up_high
            core_down[0] = down_low
            core_down[1] = down_high


def force_body(place, received, advected, up, down, forced, own, other, sums):
    core = place[0] % 2
    messages = received[...].reshape(TILES * 8, 128)
    turned = messages.T
    lon_id = lax.broadcasted_iota(jnp.int32, (LON, TILES * 8), 0).astype(F32)
    lat_id = lax.broadcasted_iota(jnp.int32, (TILES * 8, LAT), 1).astype(F32)
    total = jnp.zeros((ROWS * LON, LAT), F32)
    for g in range(4):
        here = lon_id == turned[64 + g : 65 + g, :]
        hot = jnp.where(lat_id == messages[:, 68 + g : 69 + g], 1.0, 0.0).astype(jnp.bfloat16)
        rows = turned[ROWS * g : ROWS * g + ROWS, :]
        coarse = rows.astype(jnp.bfloat16).astype(F32)
        fine = rows - coarse
        for piece in (coarse, fine):
            spread = [jnp.where(here, piece[r : r + 1, :], 0.0).astype(jnp.bfloat16) for r in range(ROWS)]
            total += jnp.dot(jnp.concatenate(spread, 0), hot, preferred_element_type=F32)
    for n in range(ROWS):
        forced[n] = advected[n] + total[n * LON : (n + 1) * LON]
    for tracer in range(TRACERS):
        rising = jnp.zeros((LON, LAT), F32)
        sinking = jnp.zeros((LON, LAT), F32)
        for lev in range(LEV_DEV):
            rising = up[lev] * (forced[tracer * LEV_DEV + lev] + rising)
        for lev in range(LEV_DEV - 1, -1, -1):
            sinking = down[lev] * (forced[tracer * LEV_DEV + lev] + sinking)
        sums[0, tracer] = rising
        sums[1, tracer] = sinking
    mine = pl.ds(pl.multiple_of(core * HALF, HALF), HALF)
    yours = pl.ds(pl.multiple_of((1 - core) * HALF, HALF), HALF)
    for way in range(2):
        for tracer in range(TRACERS):
            own[way, tracer] = sums[way, tracer, mine, :]
            other[way, tracer] = sums[way, tracer, yours, :]


def chip_body(place, own, got, core_up, core_down, blocks):
    chip = place[0] // 2
    first = place[0] % 2 == 0
    for tracer in range(TRACERS):
        rise = [jnp.where(first, own[0, tracer], got[0, tracer]), jnp.where(first, got[0, tracer], own[0, tracer])]
        sink = [jnp.where(first, own[1, tracer], got[1, tracer]), jnp.where(first, got[1, tracer], own[1, tracer])]
        rising = rise[1] + core_up[1] * rise[0]
        sinking = sink[0] + core_down[0] * sink[1]
        for to in range(4):
            blocks[to, tracer] = jnp.where(to > chip, rising, sinking)


def meet_body(place, blocks, own, got, core_up, core_down, chip_up, chip_down, keep, send):
    chip = place[0] // 2
    first = place[0] % 2 == 0
    for tracer in range(TRACERS):
        rising = jnp.zeros((HALF, LAT), F32)
        sinking = jnp.zeros((HALF, LAT), F32)
        for z in range(4):
            rising = jnp.where(z < chip, chip_up[z] * rising + blocks[z, tracer], rising)
        for z in range(3, -1, -1):
            sinking = jnp.where(z > chip, chip_down[z] * sinking + blocks[z, tracer], sinking)
        rise = jnp.where(first, own[0, tracer], got[0, tracer])
        sink = jnp.where(first, got[1, tracer], own[1, tracer])
        rising_mid = rise + core_up[0] * rising
        sinking_mid = sink + core_down[1] * sinking
        keep[0, tracer] = jnp.where(first, rising, rising_mid)
        keep[1, tracer] = jnp.where(first, sinking_mid, sinking)
        send[0, tracer] = jnp.where(first, rising_mid, rising)
        send[1, tracer] = jnp.where(first, sinking, sinking_mid)


def solve_body(place, forced, keep, got, up, down, inverse, out):
    first = place[0] % 2 == 0

    def whole(way, tracer):
        mine, yours = keep[way, tracer], got[way, tracer]
        return jnp.concatenate([jnp.where(first, mine, yours), jnp.where(first, yours, mine)], 0)

    for tracer in range(TRACERS):
        rising, sinking = whole(0, tracer), whole(1, tracer)
        partial = []
        for lev in range(LEV_DEV):
            partial.append(forced[tracer * LEV_DEV + lev] + rising)
            rising = up[lev] * partial[lev]
        for lev in range(LEV_DEV - 1, -1, -1):
            out[tracer * LEV_DEV + lev] = (partial[lev] + sinking) * inverse[lev]
            sinking = down[lev] * (forced[tracer * LEV_DEV + lev] + sinking)


def per_device(adjoint, wind_x, wind_y, kz, forcing, mon_cols, mon_counts):
    place = lax.axis_index("lev").astype(jnp.int32).reshape(1)
    field = adjoint.reshape(ROWS, LON, LAT)
    tiles = [(i, (i + 1) % TILES) for i in range(TILES)]
    cores = [(i, i ^ 1) for i in range(8)]
    chips = [[0, 2, 4, 6], [1, 3, 5, 7]]

    kz_all = lax.all_gather(kz, "lev", axis=0, tiled=True)
    payload, low, high = pack(forcing, mon_cols, mon_counts, field, wind_x)
    received = lax.all_to_all(payload, "tile", 0, 0, tiled=True)
    west = lax.ppermute(high, "tile", tiles)
    east = lax.ppermute(low, "tile", [(j, i) for i, j in tiles])

    (advected,) = call(advect_body, ((ROWS, LON, LAT),), [VMEM] * 5, moved=2 << 20)(field, wind_x, wind_y, west, east)
    level = (LEV_DEV, LON, LAT)
    pair = (2, TRACERS, HALF, LAT)
    every = pltpu.VMEM((NLEV, LON, LAT), F32)
    up, down, inverse, chip_up, chip_down, core_up, core_down = call(
        weights_body,
        (level, level, level, (4, HALF, LAT), (4, HALF, LAT), (2, HALF, LAT), (2, HALF, LAT)),
        [SMEM, VMEM],
        [every] * 4,
        moved=3 << 20,
    )(place, kz_all)
    forced, own, other = call(
        force_body,
        ((ROWS, LON, LAT), pair, pair),
        [SMEM] + [VMEM] * 4,
        [pltpu.VMEM((2, TRACERS, LON, LAT), F32)],
        limit=24 << 20,
        moved=2 << 20,
    )(place, received, advected, up, down)
    got = lax.ppermute(other, "lev", cores)
    (blocks,) = call(chip_body, ((4, TRACERS, HALF, LAT),), [SMEM] + [VMEM] * 4)(place, own, got, core_up, core_down)
    arrived = lax.all_to_all(blocks, "lev", 0, 0, tiled=True, axis_index_groups=chips)
    keep, send = call(meet_body, (pair, pair), [SMEM] + [VMEM] * 7)(
        place, arrived, own, got, core_up, core_down, chip_up, chip_down
    )
    back = lax.ppermute(send, "lev", cores)
    (updated,) = call(solve_body, ((ROWS, LON, LAT),), [SMEM] + [VMEM] * 6)(
        place, forced, keep, back, up, down, inverse
    )
    return updated.reshape(adjoint.shape)


def solution(mesh):
    in_specs = (
        P(None, "lev", "tile", None),
        P("lev", "tile", None),
        P("lev", "tile", None),
        P("lev", "tile", None),
        P("tile", None, None, "lev", None),
        P("tile", None, None),
        P("tile", None),
    )
    out_specs = P(None, "lev", "tile", None)
    return jax.shard_map(
        per_device, mesh=mesh, in_specs=in_specs, out_specs=out_specs, check_vma=False
    )
```

time: 664 us -> 87.9 us (0.13)
  the two profiles are of different devices: /device:TPU:6 before, /device:TPU:1 now
where the time goes in v1:
time: 87.9 us; the launch traced here: 86.7 us
  starting transfers between devices  41.6 us (47%)
  between operations  13.5 us (15%)
  waiting for transfers between devices  11.8 us (13%)
  blocking collectives  10.7 us (12%)
  local copies, waits for them, and re-layouts  4.6 us (5%)
  Pallas kernels  4.54 us (5%)
    all_to_all x1, starting transfers between devices, per_device(): received = lax.all_to_all(payload, 'tile', 0, 0, tiled=True)  19.7 us
    all_to_all x1, blocking collectives, per_device(): lax.all_to_all(blocks, 'lev', 0, 0, tiled=True, axis_index_groups=chips)  10.7 us
    ppermute x1, starting transfers between devices, per_device(): east = lax.ppermute(low, 'tile', [(j, i) for i, j in tiles])  10.5 us
    all_gather x1, waiting for transfers between devices, per_device(): kz_all = lax.all_gather(kz, 'lev', axis=0, tiled=True)  8.33 us
    ppermute x1, starting transfers between devices, per_device(): got = lax.ppermute(other, 'lev', cores)  5.05 us
    unnamed x16, local copies, waits for them, and re-layouts  4.6 us
    ppermute x1, starting transfers between devices, per_device(): back = lax.ppermute(send, 'lev', cores)  3.45 us
    ppermute x1, starting transfers between devices, per_device(): west = lax.ppermute(high, 'tile', tiles)  2.92 us
  transfers between devices with their start and end apart: 6, of which 4 were waited for; matrix products, arithmetic and copies ran while one was open for 0% of the time, Pallas kernels for 2%

profile of v1, /device:TPU:1, one launch (start us, length us, event | category | flops | bytes accessed | tf_op | source)
XLA Modules:
  0.0 86.7 jit_solution(9690387646172398322)
XLA Ops:
  6.5 0.0 copy-start.3
  6.5 0.0 all-gather.2.cloned.1.call-start
  6.5 0.7 all-gather.2.cloned.1.call-update
  7.3 0.0 copy-start.7
  7.3 0.2 copy-done.3
  7.4 0.5 copy-done.7
  7.9 0.0 copy-start
  7.9 1.0 %copy-done = f32[4,4,32,256]{3,2,1,0:T(8,128)S(1)} copy-done((f32[4,4,32,256]{3,2,1,0:T(8,128)S(1)}, f32[4,4,32,256]{3,2,1,0:T(8,128)}, u32[]{:S(2)}) %copy-start) | copy-done | bytes 524312
  9.0 0.0 copy-start.4
  9.0 0.9 %copy-done.4 = f32[1,64,4,4,32]{1,4,3,2,0:T(8,128)S(1)} copy-done((f32[1,64,4,4,32]{1,4,3,2,0:T(8,128)S(1)}, f32[1,64,4,4,32]{1,4,3,2,0:T(8,128)}, u32[]{:S(2)}) %copy-start.4) | copy-done | bytes 131096
  9.9 0.0 copy-start.6
  9.9 0.7 copy-done.6
  10.6 0.0 copy-start.5
  10.6 1.0 %shard_map.73 = (f32[64,8,128]{2,1,0:T(8,128)}, f32[16,256]{1,0:T(8,128)S(1)}, f32[20,256]{1,0:T(8,128)S(1)}) custom-call(f32[512,64]{1,0:T(8,128)S(1)} %bitcast.14, s32[32,64]{1,0:T(8,128)S(1)} %bitcast.15, s32[1,64]{1,0:T(1,128)S(1)} %copy-done.7, f32[16,32,256]{2,1,0:T(8,128)S(1)} %bitcast.11, f32[16,32,256]{2,1,0:T(8,128)S(1)} %bitcast.12, ...), custom_call_target="tpu_custom_call" | custom-call | bytes 1048576 | tf_op jit(solution)/shard_map/pallas_call | solution.py:63
  11.7 0.0 copy-start.1
  11.7 19.7 %all-to-all-start = ((f32[64,8,128]{2,1,0:T(8,128)}), f32[64,8,128]{2,1,0:T(8,128)S(1)}, u32[]{:S(2)}, u32[]{:S(2)}) async-start(f32[64,8,128]{2,1,0:T(8,128)} %get-tuple-element.20), calls=%async_computation | async-start | bytes 524288 | tf_op jit(solution)/shard_map/all_to_all | solution.py:232
  31.4 2.9 %collective-permute-start = (f32[20,256]{1,0:T(8,128)S(1)}, f32[20,256]{1,0:T(8,128)S(1)}, u32[]{:S(2)}, u32[]{:S(2)}) collective-permute-start(f32[20,256]{1,0:T(8,128)S(1)} %get-tuple-element.21), channel_id=1, source_target_pairs={{0,8},{8,16},{16,24},{24,32},{32,40},{40,48},{48,56},{56,64},{64,7... | collective-permute-start | bytes 61448 | tf_op jit(solution)/shard_map/ppermute | solution.py:233
  34.3 10.5 %collective-permute-start.1 = (f32[16,256]{1,0:T(8,128)S(1)}, f32[16,256]{1,0:T(8,128)S(1)}, u32[]{:S(2)}, u32[]{:S(2)}) collective-permute-start(f32[16,256]{1,0:T(8,128)S(1)} %get-tuple-element.22), channel_id=1, source_target_pairs={{8,0},{16,8},{24,16},{32,24},{40,32},{48,40},{56,48},{64,56},{72,6... | collective-permute-start | bytes 49160 | tf_op jit(solution)/shard_map/ppermute | solution.py:234
  44.8 0.8 collective-permute-done.1.east
  45.6 0.0 collective-permute-done.west
  45.6 0.0 copy-done.5
  45.6 0.0 copy-done.1
  45.7 0.4 shard_map.74.advected
  46.1 8.3 %all-gather.2.cloned.1.call-done.kz = f32[32,32,256]{2,1,0:T(8,128)} async-done(((f32[4,32,256]{2,1,0:T(8,128)}), f32[32,32,256]{2,1,0:T(8,128)}) %all-gather.2.cloned.1.call-update) | async-done | bytes 1048592 | tf_op jit(solution)/shard_map/all_gather | solution.py:230
  54.4 0.0 copy-start.2
  54.4 1.2 %copy-done.2 = f32[32,32,256]{2,1,0:T(8,128)S(1)} copy-done((f32[32,32,256]{2,1,0:T(8,128)S(1)}, f32[32,32,256]{2,1,0:T(8,128)}, u32[]{:S(2)}) %copy-start.2) | copy-done | bytes 1048600
  55.6 0.5 shard_map.75
  56.1 0.0 all-to-all-done.received
  56.1 1.5 %shard_map.76 = (f32[16,32,256]{2,1,0:T(8,128)S(1)}, f32[2,4,16,256]{3,2,1,0:T(8,128)S(1)}, f32[2,4,16,256]{3,2,1,0:T(8,128)S(1)}) custom-call(s32[1]{0:T(128)} %bitcast.place, f32[64,8,128]{2,1,0:T(8,128)S(1)} %all-to-all-done.received, f32[16,32,256]{2,1,0:T(8,128)S(1)} %shard_map.74.advected, f32[4,32,256]{2,1,0:T(8,128)S(1)} %get-tuple-element.23.up, ...), custom_call_target="tpu_custom_call" | custom-call | bytes 2097152 | tf_op jit(solution)/shard_map/pallas_call | solution.py:247
  57.7 5.1 %collective-permute-start.2 = (f32[2,4,16,256]{3,2,1,0:T(8,128)S(1)}, f32[2,4,16,256]{3,2,1,0:T(8,128)S(1)}, u32[]{:S(2)}, u32[]{:S(2)}) collective-permute-start(f32[2,4,16,256]{3,2,1,0:T(8,128)S(1)} %get-tuple-element.27), channel_id=1, source_target_pairs={{0,1},{1,0},{2,3},{3,2},{4,5},{5,4},{6,7},{7,6},{8,9},{9,8},{10,11... | collective-permute-start | bytes 393224 | tf_op jit(solution)/shard_map/ppermute | solution.py:255
  62.7 1.0 %collective-permute-done.2.got = f32[2,4,16,256]{3,2,1,0:T(8,128)S(1)} collective-permute-done((f32[2,4,16,256]{3,2,1,0:T(8,128)S(1)}, f32[2,4,16,256]{3,2,1,0:T(8,128)S(1)}, u32[]{:S(2)}, u32[]{:S(2)}) %collective-permute-start.2) | collective-permute-done | bytes 131104 | tf_op jit(solution)/shard_map/ppermute | solution.py:255
  63.7 10.7 %all_to_all.10.blocks = f32[4,4,16,256]{3,2,1,0:T(8,128)S(1)} all-to-all(f32[4,4,16,256]{3,2,1,0:T(8,128)S(1)} %shard_map.77), channel_id=1, replica_groups={{0,2,4,6},{1,3,5,7},{8,10,12,14},{9,11,13,15},{16,18,20,22},{17,19,21,2..., dimensions={0} | all-to-all | bytes 524288 | tf_op jit(solution)/shard_map/all_to_all | solution.py:257
  74.4 0.1 shard_map.78
  74.5 3.4 %collective-permute-start.3 = (f32[2,4,16,256]{3,2,1,0:T(8,128)S(1)}, f32[2,4,16,256]{3,2,1,0:T(8,128)S(1)}, u32[]{:S(2)}, u32[]{:S(2)}) collective-permute-start(f32[2,4,16,256]{3,2,1,0:T(8,128)S(1)} %get-tuple-element.33), channel_id=1, source_target_pairs={{0,1},{1,0},{2,3},{3,2},{4,5},{5,4},{6,7},{7,6},{8,9},{9,8},{10,11... | collective-permute-start | bytes 393224 | tf_op jit(solution)/shard_map/ppermute | solution.py:261
  78.0 1.0 %collective-permute-done.3.got = f32[2,4,16,256]{3,2,1,0:T(8,128)S(1)} collective-permute-done((f32[2,4,16,256]{3,2,1,0:T(8,128)S(1)}, f32[2,4,16,256]{3,2,1,0:T(8,128)S(1)}, u32[]{:S(2)}, u32[]{:S(2)}) %collective-permute-start.3) | collective-permute-done | bytes 131104 | tf_op jit(solution)/shard_map/ppermute | solution.py:261
  79.0 0.9 %shard_map.79 = f32[16,32,256]{2,1,0:T(8,128)} custom-call(s32[1]{0:T(128)} %bitcast.place, f32[16,32,256]{2,1,0:T(8,128)S(1)} %get-tuple-element.25.forced, f32[2,4,16,256]{3,2,1,0:T(8,128)S(1)} %get-tuple-element.32.keep, f32[2,4,16,256]{3,2,1,0:T(8,128)S(1)} %collective-permute-done.3.got, f32[4,32,256]{2,1,0:T(8,128)S(1)} %get-tuple-element.23.up, ...), custom_call_target="tpu_custom_call" | custom-call | bytes 1048576 | tf_op jit(solution)/shard_map/pallas_call | solution.py:262
  (1 shorter events, 0.0 us)
Async XLA Ops:
  6.5 0.9 %copy-start.3 = (f32[4,32,256]{2,1,0:T(8,128)S(1)}, f32[4,32,256]{2,1,0:T(8,128)}, u32[]{:S(2)}) copy-start(f32[4,32,256]{2,1,0:T(8,128)} %wind_x.1) | copy-start | bytes 393220
  6.5 47.9 %all-gather.2.cloned.1.call-start = ((), (), s32[]{:S(2)}) async-start(), calls=%async_computation.2 | async-start | bytes 1179648 | tf_op jit(solution)/shard_map/all_gather | solution.py:230
  7.3 0.7 copy-start.7
  7.9 1.0 %copy-start = (f32[4,4,32,256]{3,2,1,0:T(8,128)S(1)}, f32[4,4,32,256]{3,2,1,0:T(8,128)}, u32[]{:S(2)}) copy-start(f32[4,4,32,256]{3,2,1,0:T(8,128)} %param.7) | copy-start | bytes 1572868
  9.0 0.9 %copy-start.4 = (f32[1,64,4,4,32]{1,4,3,2,0:T(8,128)S(1)}, f32[1,64,4,4,32]{1,4,3,2,0:T(8,128)}, u32[]{:S(2)}) copy-start(f32[1,64,4,4,32]{1,4,3,2,0:T(8,128)} %param.11) | copy-start | bytes 393220
  9.9 0.7 copy-start.6
  10.6 35.0 %copy-start.5 = (f32[4,32,256]{2,1,0:T(8,128)S(1)}, f32[4,32,256]{2,1,0:T(8,128)}, u32[]{:S(2)}) copy-start(f32[4,32,256]{2,1,0:T(8,128)} %wind_y.1) | copy-start | bytes 393220
  11.7 34.0 %copy-start.1 = (f32[4,4,32,256]{3,2,1,0:T(8,128)S(1)}, f32[4,4,32,256]{3,2,1,0:T(8,128)}, u32[]{:S(2)}) copy-start(f32[4,4,32,256]{3,2,1,0:T(8,128)} %param.7) | copy-start | bytes 1572868
  11.7 44.5 %all-to-all-start = ((f32[64,8,128]{2,1,0:T(8,128)}), f32[64,8,128]{2,1,0:T(8,128)S(1)}, u32[]{:S(2)}, u32[]{:S(2)}) async-start(f32[64,8,128]{2,1,0:T(8,128)} %get-tuple-element.20), calls=%async_computation | async-start | bytes 524288 | tf_op jit(solution)/shard_map/all_to_all | solution.py:232
  31.4 14.3 %collective-permute-start = (f32[20,256]{1,0:T(8,128)S(1)}, f32[20,256]{1,0:T(8,128)S(1)}, u32[]{:S(2)}, u32[]{:S(2)}) collective-permute-start(f32[20,256]{1,0:T(8,128)S(1)} %get-tuple-element.21), channel_id=1, source_target_pairs={{0,8},{8,16},{16,24},{24,32},{32,40},{40,48},{48,56},{56,64},{64,7... | collective-permute-start | bytes 61448 | tf_op jit(solution)/shard_map/ppermute | solution.py:233
  34.3 11.3 %collective-permute-start.1 = (f32[16,256]{1,0:T(8,128)S(1)}, f32[16,256]{1,0:T(8,128)S(1)}, u32[]{:S(2)}, u32[]{:S(2)}) collective-permute-start(f32[16,256]{1,0:T(8,128)S(1)} %get-tuple-element.22), channel_id=1, source_target_pairs={{8,0},{16,8},{24,16},{32,24},{40,32},{48,40},{56,48},{64,56},{72,6... | collective-permute-start | bytes 49160 | tf_op jit(solution)/shard_map/ppermute | solution.py:234
  54.4 1.2 %copy-start.2 = (f32[32,32,256]{2,1,0:T(8,128)S(1)}, f32[32,32,256]{2,1,0:T(8,128)}, u32[]{:S(2)}) copy-start(f32[32,32,256]{2,1,0:T(8,128)} %all-gather.2.cloned.1.call-done.kz) | copy-start | bytes 3145732
  57.7 6.0 %collective-permute-start.2 = (f32[2,4,16,256]{3,2,1,0:T(8,128)S(1)}, f32[2,4,16,256]{3,2,1,0:T(8,128)S(1)}, u32[]{:S(2)}, u32[]{:S(2)}) collective-permute-start(f32[2,4,16,256]{3,2,1,0:T(8,128)S(1)} %get-tuple-element.27), channel_id=1, source_target_pairs={{0,1},{1,0},{2,3},{3,2},{4,5},{5,4},{6,7},{7,6},{8,9},{9,8},{10,11... | collective-permute-start | bytes 393224 | tf_op jit(solution)/shard_map/ppermute | solution.py:255
  74.5 4.4 %collective-permute-start.3 = (f32[2,4,16,256]{3,2,1,0:T(8,128)S(1)}, f32[2,4,16,256]{3,2,1,0:T(8,128)S(1)}, u32[]{:S(2)}, u32[]{:S(2)}) collective-permute-start(f32[2,4,16,256]{3,2,1,0:T(8,128)S(1)} %get-tuple-element.33), channel_id=1, source_target_pairs={{0,1},{1,0},{2,3},{3,2},{4,5},{5,4},{6,7},{7,6},{8,9},{9,8},{10,11... | collective-permute-start | bytes 393224 | tf_op jit(solution)/shard_map/ppermute | solution.py:261
Sparse Core Ops, SparseCore 0:
  9.4 44.9 all-gather.1

commit v2 on v0

v2 whole, which is shorter than its diff:
```python
import jax
import jax.numpy as jnp
from jax import lax
from jax.experimental import pallas as pl
from jax.experimental.pallas import tpu as pltpu
from jax.sharding import PartitionSpec as P

TRACERS = 4
LEV_DEV = 4
LEVS = 8
NLEV = 32
LON = 32
LAT = 256
TILES = 64
CAP = 32
HALF = LON // 2
ROWS = TRACERS * LEV_DEV
VMEM = pl.BlockSpec(memory_space=pltpu.VMEM)
HBM = pl.BlockSpec(memory_space=pltpu.HBM)
SMEM = pl.BlockSpec(memory_space=pltpu.SMEM)
F32 = jnp.float32


def call(body, outs, in_specs, scratch=(), limit=12 << 20, flops=0, moved=1 << 20, **more):
    shapes = tuple(jax.ShapeDtypeStruct(shape, F32) for shape in outs)
    return pl.pallas_call(
        body,
        out_shape=shapes,
        in_specs=in_specs,
        out_specs=tuple(VMEM for _ in outs),
        scratch_shapes=list(scratch),
        compiler_params=pltpu.CompilerParams(vmem_limit_bytes=limit),
        cost_estimate=pl.CostEstimate(flops=flops, bytes_accessed=moved, transcendentals=0),
        **more,
    )


def pack_body(place, force, cols, counts, adj, wind, payload, first, second, force_v, cols_v, counts_v, low_v, high_v, wind_v, sems):
    last = pl.ds(LON - 8, 8)
    copies = [
        pltpu.make_async_copy(force, force_v, sems.at[0]),
        pltpu.make_async_copy(cols, cols_v, sems.at[1]),
        pltpu.make_async_copy(counts, counts_v, sems.at[2]),
        pltpu.make_async_copy(adj.at[:, pl.ds(0, 8), :], low_v, sems.at[3]),
        pltpu.make_async_copy(adj.at[:, last, :], high_v, sems.at[4]),
        pltpu.make_async_copy(wind.at[:, last, :], wind_v, sems.at[5]),
    ]
    for copy in copies:
        copy.start()
    for copy in copies:
        copy.wait()
    for k in range(4):
        parts = [force_v[pl.ds(8 * k + g, ROWS, stride=CAP), :] for g in range(8)]
        payload[:, 0, 128 * k : 128 * (k + 1)] = jnp.concatenate(parts, 0).T
    slot = lax.broadcasted_iota(jnp.int32, (CAP, TILES), 0)
    lon = jnp.where(slot < counts_v[...], cols_v[...] >> 8, -1).astype(F32)
    lat = (cols_v[...] & 255).astype(F32)
    payload[:, 0, 512:640] = jnp.concatenate([lon, lat, jnp.zeros((64, TILES), F32)], 0).T
    even = place[0] % 2 == 0
    low, high, cx = low_v[:, 0, :], high_v[:, 7, :], wind_v[:, 7, :]
    first[0:ROWS, :] = jnp.where(even, high, low)
    second[0:ROWS, :] = jnp.where(even, low, high)
    first[ROWS : ROWS + LEV_DEV, :] = cx
    second[ROWS : ROWS + LEV_DEV, :] = cx


def pack(tile, forcing, mon_cols, mon_counts, field, wind_x):
    force = jnp.transpose(forcing[0], (1, 2, 3, 0)).reshape(ROWS * CAP, TILES)
    cols = jnp.transpose(mon_cols[0], (1, 0))
    edge = (ROWS + LEV_DEV, LAT)
    scratch = [
        pltpu.VMEM((ROWS * CAP, TILES), F32),
        pltpu.VMEM((CAP, TILES), jnp.int32),
        pltpu.VMEM((1, TILES), jnp.int32),
        pltpu.VMEM((ROWS, 8, LAT), F32),
        pltpu.VMEM((ROWS, 8, LAT), F32),
        pltpu.VMEM((LEV_DEV, 8, LAT), F32),
        pltpu.SemaphoreType.DMA((6,)),
    ]
    operands = [pltpu.with_memory_space_constraint(x, pltpu.HBM) for x in (force, cols, mon_counts, field, wind_x)]
    return call(pack_body, ((TILES, 1, 640), edge, edge), [SMEM] + [HBM] * 5, scratch)(tile, *operands)


def advect_body(place, adj, wind_x, wind_y, first, second, out):
    even = place[0] % 2 == 0
    west = jnp.where(even, second[...], first[...])
    east = jnp.where(even, first[...], second[...])
    row = lax.broadcasted_iota(jnp.int32, (LON, LAT), 0)
    lane = lax.broadcasted_iota(jnp.int32, (LON, LAT), 1)
    for lev in range(LEV_DEV):
        cx = wind_x[lev]
        cx_west = jnp.where(row == 0, west[ROWS + lev : ROWS + lev + 1, :], pltpu.roll(cx, 1, 0))
        cy_n = jnp.where(lane == LAT - 1, 0.0, wind_y[lev])
        cy_s = pltpu.roll(cy_n, 1, 1)
        to_east = jnp.maximum(cx, 0.0)
        to_west = jnp.minimum(cx_west, 0.0)
        to_north = jnp.maximum(cy_n, 0.0)
        to_south = jnp.minimum(cy_s, 0.0)
        for tracer in range(TRACERS):
            n = tracer * LEV_DEV + lev
            a = adj[n]
            a_east = jnp.where(row == LON - 1, east[n : n + 1, :], pltpu.roll(a, LON - 1, 0))
            a_west = jnp.where(row == 0, west[n : n + 1, :], pltpu.roll(a, 1, 0))
            a_north = pltpu.roll(a, LAT - 1, 1)
            a_south = pltpu.roll(a, 1, 1)
            out[n] = (
                a
                + to_east * (a_east - a)
                - to_west * (a_west - a)
                + to_north * (a_north - a)
                - to_south * (a_south - a)
            )


def block_body(place, kz, carry, ports):
    shunt = jnp.ones((LON, LAT), F32)
    series = kz[0]
    top = jnp.zeros((LON, LAT), F32)
    for lev in range(1, LEV_DEV):
        k = kz[lev]
        if lev == LEV_DEV - 1:
            k = jnp.where(place[0] == LEVS - 1, 0.0, k)
        ground = 1.0 + top
        inverse = 1.0 / (series + k + ground)
        below, above = series * inverse, k * inverse
        carry[0, lev - 1] = below
        carry[1, lev - 1] = above
        carry[2, lev - 1] = inverse
        shunt = shunt + below * ground
        top = above * ground
        series = below * k
    ports[0] = shunt
    ports[1] = series
    ports[2] = top


def chunks(array):
    return [array[8 * (w // 2) : 8 * (w // 2) + 8, 128 * (w % 2) : 128 * (w % 2) + 128] for w in range(LEVS)]


def force_body(received, advected, carry, ports, inner, blocks):
    data = jnp.concatenate([received[:, 0, 128 * k : 128 * (k + 1)] for k in range(4)], 0)
    where = received[:, 0, 512:640]
    where = jnp.concatenate([where] + [pltpu.roll(where, 128 - 8 * k, 1) for k in range(1, 4)], 0)
    rows_all, lons = data.T, where.T
    lon_id = lax.broadcasted_iota(jnp.int32, (LON, 4 * TILES), 0).astype(F32)
    lat_id = lax.broadcasted_iota(jnp.int32, (4 * TILES, LAT), 1).astype(F32)
    total = jnp.zeros((ROWS * LON, LAT), F32)
    for g in range(8):
        here = lon_id == lons[g : g + 1, :]
        hot = jnp.where(lat_id == where[:, CAP + g : CAP + g + 1], 1.0, 0.0).astype(jnp.bfloat16)
        rows = rows_all[ROWS * g : ROWS * g + ROWS, :]
        coarse = rows.astype(jnp.bfloat16).astype(F32)
        fine = rows - coarse
        for piece in (coarse, fine):
            spread = [jnp.where(here, piece[r : r + 1, :], 0.0).astype(jnp.bfloat16) for r in range(ROWS)]
            total += jnp.dot(jnp.concatenate(spread, 0), hot, preferred_element_type=F32)
    for tracer in range(TRACERS):
        forced = []
        for lev in range(LEV_DEV):
            n = tracer * LEV_DEV + lev
            forced.append(advected[n] + total[n * LON : (n + 1) * LON])
        low = forced[0]
        high = jnp.zeros((LON, LAT), F32)
        for lev in range(1, LEV_DEV):
            middle = high + forced[lev]
            low = low + carry[0, lev - 1] * middle
            high = carry[1, lev - 1] * middle
            inner[tracer, lev - 1] = carry[2, lev - 1] * middle
        for w, (piece_low, piece_high) in enumerate(zip(chunks(low), chunks(high))):
            blocks[w, tracer] = piece_low
            blocks[w, TRACERS + tracer] = piece_high
    for n in range(3):
        for w, piece in enumerate(chunks(ports[n])):
            blocks[w, 2 * TRACERS + n] = piece


def chain_body(blocks, ends):
    zero = jnp.zeros((8, 128), F32)
    below, rising = [zero], [[zero] * TRACERS]
    for p in range(LEVS - 1):
        shunt, series, top = [blocks[p, 2 * TRACERS + n] for n in range(3)]
        ground = shunt + below[p]
        share = series / (series + ground)
        below.append(top + share * ground)
        rising.append([blocks[p, TRACERS + t] + share * (blocks[p, t] + rising[p][t]) for t in range(TRACERS)])
    above, sinking = zero, [zero] * TRACERS
    for p in range(LEVS - 1, -1, -1):
        shunt, series, top = [blocks[p, 2 * TRACERS + n] for n in range(3)]
        if p == LEVS - 1:
            above, sinking = shunt, [blocks[p, t] for t in range(TRACERS)]
        else:
            ground = top + above
            share = series / (series + ground)
            above = shunt + share * ground
            sinking = [blocks[p, t] + share * (blocks[p, TRACERS + t] + sinking[t]) for t in range(TRACERS)]
        inverse = 1.0 / (below[p] + above)
        for t in range(TRACERS):
            value = (rising[p][t] + sinking[t]) * inverse
            ends[p, t] = value
            if p > 0:
                ends[p - 1, TRACERS + t] = value
            if p == LEVS - 1:
                ends[p, TRACERS + t] = zero


def solve_body(inner, ends, carry, out):
    def whole(n):
        return jnp.concatenate([jnp.concatenate([ends[2 * a, n], ends[2 * a + 1, n]], 1) for a in range(4)], 0)

    for tracer in range(TRACERS):
        bottom, level = whole(tracer), whole(TRACERS + tracer)
        for lev in range(LEV_DEV - 1, 0, -1):
            level = inner[tracer, lev - 1] + carry[0, lev - 1] * bottom + carry[1, lev - 1] * level
            out[tracer * LEV_DEV + lev] = level
        out[tracer * LEV_DEV] = bottom


def per_device(adjoint, wind_x, wind_y, kz, forcing, mon_cols, mon_counts):
    place = lax.axis_index("lev").astype(jnp.int32).reshape(1)
    tile = lax.axis_index("tile").astype(jnp.int32).reshape(1)
    field = adjoint.reshape(ROWS, LON, LAT)
    inside = (LEV_DEV - 1, LON, LAT)

    payload, first, second = pack(tile, forcing, mon_cols, mon_counts, field, wind_x)
    received = lax.all_to_all(payload, "tile", 0, 0, tiled=True)
    first = lax.ppermute(first, "tile", [(i, i ^ 1) for i in range(TILES)])
    second = lax.ppermute(second, "tile", [(i, (i + 1 if i % 2 else i - 1) % TILES) for i in range(TILES)])
    carry, ports = call(block_body, ((3,) + inside, (3, LON, LAT)), [SMEM, VMEM])(place, kz)
    (advected,) = call(advect_body, ((ROWS, LON, LAT),), [SMEM] + [VMEM] * 5, moved=2 << 20)(
        tile, field, wind_x, wind_y, first, second
    )
    inner, blocks = call(
        force_body,
        ((TRACERS,) + inside, (LEVS, 11, 8, 128)),
        [VMEM] * 4,
        limit=24 << 20,
        moved=2 << 20,
    )(received, advected, carry, ports)
    arrived = lax.all_to_all(blocks, "lev", 0, 0, tiled=True)
    (ends,) = call(chain_body, ((LEVS, 2 * TRACERS, 8, 128),), [VMEM])(arrived)
    ends = lax.all_to_all(ends, "lev", 0, 0, tiled=True)
    (updated,) = call(solve_body, ((ROWS, LON, LAT),), [VMEM] * 3)(inner, ends, carry)
    return updated.reshape(adjoint.shape)


def solution(mesh):
    in_specs = (
        P(None, "lev", "tile", None),
        P("lev", "tile", None),
        P("lev", "tile", None),
        P("lev", "tile", None),
        P("tile", None, None, "lev", None),
        P("tile", None, None),
        P("tile", None),
    )
    out_specs = P(None, "lev", "tile", None)
    return jax.shard_map(
        per_device, mesh=mesh, in_specs=in_specs, out_specs=out_specs, check_vma=False
    )
```

time: 664 us -> 70.9 us (0.11)
  the two profiles are of different devices: /device:TPU:6 before, /device:TPU:1 now
where the time goes in v2:
time: 70.9 us; the launch traced here: 70.5 us
  starting transfers between devices  33.7 us (48%)
  blocking collectives  29.7 us (42%)
  Pallas kernels  5.04 us (7%)
  waiting for transfers between devices  1.95 us (3%)
    all_to_all x1, starting transfers between devices, per_device(): received = lax.all_to_all(payload, 'tile', 0, 0, tiled=True)  19.7 us
    all_to_all x1, blocking collectives, per_device(): arrived = lax.all_to_all(blocks, 'lev', 0, 0, tiled=True)  17.8 us
    all_to_all x1, blocking collectives, per_device(): ends = lax.all_to_all(ends, 'lev', 0, 0, tiled=True)  11.9 us
    ppermute x1, starting transfers between devices, per_device(): lax.ppermute(second, 'tile', [(i, (i + 1 if i % 2 else i - 1) % TILES) fo...  10.9 us
    ppermute x1, starting transfers between devices, per_device(): first = lax.ppermute(first, 'tile', [(i, i ^ 1) for i in range(TILES)])  3.05 us
    pallas_call x1, Pallas kernels, pack(): call(pack_body, ((TILES, 1, 640), edge, edge), [SMEM] + [HBM] * 5, scratch)  2.11 us
    ppermute x1, waiting for transfers between devices, per_device(): lax.ppermute(second, 'tile', [(i, (i + 1 if i % 2 else i - 1) % TILES) fo...  1.94 us
    pallas_call x1, Pallas kernels, per_device(): call(force_body, ((TRACERS,) + inside, (LEVS, 11, 8, 128)), [VMEM] * 4, l...  1.5 us
  transfers between devices with their start and end apart: 3, of which 1 were waited for; matrix products, arithmetic and copies ran while one was open for 0% of the time, Pallas kernels for 1%

profile of v2, /device:TPU:1, one launch (start us, length us, event | category | flops | bytes accessed | tf_op | source)
XLA Modules:
  0.0 70.5 jit_solution(16677314071667529137)
XLA Ops:
  0.0 0.0 copy-start
  0.0 2.1 %shard_map.73 = (f32[64,1,640]{2,1,0:T(1,128)}, f32[20,256]{1,0:T(8,128)S(1)}, f32[20,256]{1,0:T(8,128)S(1)}) custom-call(s32[1]{0:T(128)} %bitcast.place, f32[512,64]{1,0:T(8,128)} %bitcast.14, s32[32,64]{1,0:T(8,128)} %bitcast.15, s32[1,64]{1,0:T(1,128)} %counts.1, f32[16,32,256]{2,1,0:T(8,128)} %bitcast.12, f32[4,32,256]{2,1,0:T(8,128)} %wind_x.1), custom_call_target="tpu_custom_call" | custom-call | bytes 1048576 | tf_op jit(solution)/shard_map/pallas_call | solution.py:81
  2.1 0.0 copy-start.3
  2.1 0.0 copy-start.2
  2.1 19.7 %all-to-all-start = ((f32[64,1,640]{2,1,0:T(1,128)}), f32[64,1,640]{2,1,0:T(1,128)S(1)}, u32[]{:S(2)}, u32[]{:S(2)}) async-start(f32[64,1,640]{2,1,0:T(1,128)} %get-tuple-element.12), calls=%async_computation | async-start | bytes 327680 | tf_op jit(solution)/shard_map/all_to_all | solution.py:226
  21.9 0.0 copy-start.1
  21.9 3.1 %collective-permute-start = (f32[20,256]{1,0:T(8,128)S(1)}, f32[20,256]{1,0:T(8,128)S(1)}, u32[]{:S(2)}, u32[]{:S(2)}) collective-permute-start(f32[20,256]{1,0:T(8,128)S(1)} %get-tuple-element.13), channel_id=1, source_target_pairs={{0,8},{8,0},{16,24},{24,16},{32,40},{40,32},{48,56},{56,48},{64,72... | collective-permute-start | bytes 61448 | tf_op jit(solution)/shard_map/ppermute | solution.py:227
  24.9 10.9 %collective-permute-start.1 = (f32[20,256]{1,0:T(8,128)S(1)}, f32[20,256]{1,0:T(8,128)S(1)}, u32[]{:S(2)}, u32[]{:S(2)}) collective-permute-start(f32[20,256]{1,0:T(8,128)S(1)} %get-tuple-element.14), channel_id=1, source_target_pairs={{0,504},{8,16},{16,8},{24,32},{32,24},{40,48},{48,40},{56,64},{64,... | collective-permute-start | bytes 61448 | tf_op jit(solution)/shard_map/ppermute | solution.py:228
  35.9 0.0 copy-done.3
  35.9 0.0 collective-permute-done.first
  35.9 1.9 %collective-permute-done.1.second = f32[20,256]{1,0:T(8,128)S(1)} collective-permute-done((f32[20,256]{1,0:T(8,128)S(1)}, f32[20,256]{1,0:T(8,128)S(1)}, u32[]{:S(2)}, u32[]{:S(2)}) %collective-permute-start.1) | collective-permute-done | bytes 20512 | tf_op jit(solution)/shard_map/ppermute | solution.py:228
  37.9 0.0 copy-done
  37.9 0.0 copy-done.2
  37.9 0.0 copy-done.1
  37.9 0.4 shard_map.74.advected
  38.3 0.0 all-to-all-done.received
  38.3 1.5 %shard_map.76 = (f32[4,3,32,256]{3,2,1,0:T(8,128)S(1)}, f32[8,11,8,128]{3,2,1,0:T(8,128)S(1)}) custom-call(f32[64,1,640]{2,1,0:T(1,128)S(1)} %all-to-all-done.received, f32[16,32,256]{2,1,0:T(8,128)S(1)} %shard_map.74.advected, f32[3,3,32,256]{3,2,1,0:T(8,128)S(1)} %get-tuple-element.15.carry, f32[3,32,256]{2,1,0:T(8,128)S(1)} %get-tuple-element.16.ports), custom_call_target="tpu_custom_call" | custom-call | bytes 2097152 | tf_op jit(solution)/shard_map/pallas_call | solution.py:233
  39.8 17.8 %all_to_all.15.blocks = f32[8,11,8,128]{3,2,1,0:T(8,128)S(1)} all-to-all(f32[8,11,8,128]{3,2,1,0:T(8,128)S(1)} %get-tuple-element.18), channel_id=1, replica_groups=mesh['tile'=64,'lev'=8] {'lev'}, dimensions={0} | all-to-all | bytes 720896 | tf_op jit(solution)/shard_map/all_to_all | solution.py:240
  57.7 0.1 shard_map.77
  57.8 11.9 %all_to_all.16.ends = f32[8,8,8,128]{3,2,1,0:T(8,128)S(1)} all-to-all(f32[8,8,8,128]{3,2,1,0:T(8,128)S(1)} %shard_map.77), channel_id=1, replica_groups=mesh['tile'=64,'lev'=8] {'lev'}, dimensions={0} | all-to-all | bytes 524288 | tf_op jit(solution)/shard_map/all_to_all | solution.py:242
  69.7 0.9 %shard_map.78 = f32[16,32,256]{2,1,0:T(8,128)} custom-call(f32[4,3,32,256]{3,2,1,0:T(8,128)S(1)} %get-tuple-element.17.inner, f32[8,8,8,128]{3,2,1,0:T(8,128)S(1)} %all_to_all.16.ends, f32[3,3,32,256]{3,2,1,0:T(8,128)S(1)} %get-tuple-element.15.carry), custom_call_target="tpu_custom_call" | custom-call | bytes 1048576 | tf_op jit(solution)/shard_map/pallas_call | solution.py:243
  (1 shorter events, 0.0 us)
Async XLA Ops:
  0.0 37.9 %copy-start = (f32[4,4,32,256]{3,2,1,0:T(8,128)S(1)}, f32[4,4,32,256]{3,2,1,0:T(8,128)}, u32[]{:S(2)}) copy-start(f32[4,4,32,256]{3,2,1,0:T(8,128)} %param.7) | copy-start | bytes 1572868
  2.1 33.7 %copy-start.3 = (f32[4,32,256]{2,1,0:T(8,128)S(1)}, f32[4,32,256]{2,1,0:T(8,128)}, u32[]{:S(2)}) copy-start(f32[4,32,256]{2,1,0:T(8,128)} %kz.1) | copy-start | bytes 393220
  2.1 35.7 %copy-start.2 = (f32[4,32,256]{2,1,0:T(8,128)S(1)}, f32[4,32,256]{2,1,0:T(8,128)}, u32[]{:S(2)}) copy-start(f32[4,32,256]{2,1,0:T(8,128)} %wind_y.1) | copy-start | bytes 393220
  2.1 36.2 %all-to-all-start = ((f32[64,1,640]{2,1,0:T(1,128)}), f32[64,1,640]{2,1,0:T(1,128)S(1)}, u32[]{:S(2)}, u32[]{:S(2)}) async-start(f32[64,1,640]{2,1,0:T(1,128)} %get-tuple-element.12), calls=%async_computation | async-start | bytes 327680 | tf_op jit(solution)/shard_map/all_to_all | solution.py:226
  21.9 16.0 %copy-start.1 = (f32[4,32,256]{2,1,0:T(8,128)S(1)}, f32[4,32,256]{2,1,0:T(8,128)}, u32[]{:S(2)}) copy-start(f32[4,32,256]{2,1,0:T(8,128)} %wind_x.1) | copy-start | bytes 393220
  21.9 14.1 %collective-permute-start = (f32[20,256]{1,0:T(8,128)S(1)}, f32[20,256]{1,0:T(8,128)S(1)}, u32[]{:S(2)}, u32[]{:S(2)}) collective-permute-start(f32[20,256]{1,0:T(8,128)S(1)} %get-tuple-element.13), channel_id=1, source_target_pairs={{0,8},{8,0},{16,24},{24,16},{32,40},{40,32},{48,56},{56,48},{64,72... | collective-permute-start | bytes 61448 | tf_op jit(solution)/shard_map/ppermute | solution.py:227
  24.9 12.9 %collective-permute-start.1 = (f32[20,256]{1,0:T(8,128)S(1)}, f32[20,256]{1,0:T(8,128)S(1)}, u32[]{:S(2)}, u32[]{:S(2)}) collective-permute-start(f32[20,256]{1,0:T(8,128)S(1)} %get-tuple-element.14), channel_id=1, source_target_pairs={{0,504},{8,16},{16,8},{24,32},{32,24},{40,48},{48,40},{56,64},{64,... | collective-permute-start | bytes 61448 | tf_op jit(solution)/shard_map/ppermute | solution.py:228

commit v3 on v2

--- a/solution.py
+++ b/solution.py
@@ -21,13 +21,13 @@
 F32 = jnp.float32
 
 
-def call(body, outs, in_specs, scratch=(), limit=12 << 20, flops=0, moved=1 << 20, **more):
+def call(body, outs, in_specs, scratch=(), limit=12 << 20, flops=0, moved=1 << 20, out_spec=VMEM, **more):
     shapes = tuple(jax.ShapeDtypeStruct(shape, F32) for shape in outs)
     return pl.pallas_call(
         body,
         out_shape=shapes,
         in_specs=in_specs,
-        out_specs=tuple(VMEM for _ in outs),
+        out_specs=tuple(out_spec for _ in outs),
         scratch_shapes=list(scratch),
         compiler_params=pltpu.CompilerParams(vmem_limit_bytes=limit),
         cost_estimate=pl.CostEstimate(flops=flops, bytes_accessed=moved, transcendentals=0),
@@ -51,11 +51,11 @@
         copy.wait()
     for k in range(4):
         parts = [force_v[pl.ds(8 * k + g, ROWS, stride=CAP), :] for g in range(8)]
-        payload[:, 0, 128 * k : 128 * (k + 1)] = jnp.concatenate(parts, 0).T
+        payload[pl.ds(k, TILES, stride=5), :] = jnp.concatenate(parts, 0).T
     slot = lax.broadcasted_iota(jnp.int32, (CAP, TILES), 0)
     lon = jnp.where(slot < counts_v[...], cols_v[...] >> 8, -1).astype(F32)
     lat = (cols_v[...] & 255).astype(F32)
-    payload[:, 0, 512:640] = jnp.concatenate([lon, lat, jnp.zeros((64, TILES), F32)], 0).T
+    payload[pl.ds(4, TILES, stride=5), :] = jnp.concatenate([lon, lat, jnp.zeros((64, TILES), F32)], 0).T
     even = place[0] % 2 == 0
     low, high, cx = low_v[:, 0, :], high_v[:, 7, :], wind_v[:, 7, :]
     first[0:ROWS, :] = jnp.where(even, high, low)
@@ -78,37 +78,29 @@
         pltpu.SemaphoreType.DMA((6,)),
     ]
     operands = [pltpu.with_memory_space_constraint(x, pltpu.HBM) for x in (force, cols, mon_counts, field, wind_x)]
-    return call(pack_body, ((TILES, 1, 640), edge, edge), [SMEM] + [HBM] * 5, scratch)(tile, *operands)
-
-
-def advect_body(place, adj, wind_x, wind_y, first, second, out):
-    even = place[0] % 2 == 0
-    west = jnp.where(even, second[...], first[...])
-    east = jnp.where(even, first[...], second[...])
+    return call(pack_body, ((TILES * 5, 128), edge, edge), [SMEM] + [HBM] * 5, scratch)(tile, *operands)
+
+
+def advect_body(adj, wind_x, wind_y, out):
     row = lax.broadcasted_iota(jnp.int32, (LON, LAT), 0)
     lane = lax.broadcasted_iota(jnp.int32, (LON, LAT), 1)
     for lev in range(LEV_DEV):
         cx = wind_x[lev]
-        cx_west = jnp.where(row == 0, west[ROWS + lev : ROWS + lev + 1, :], pltpu.roll(cx, 1, 0))
         cy_n = jnp.where(lane == LAT - 1, 0.0, wind_y[lev])
         cy_s = pltpu.roll(cy_n, 1, 1)
-        to_east = jnp.maximum(cx, 0.0)
-        to_west = jnp.minimum(cx_west, 0.0)
+        to_east = jnp.where(row == LON - 1, 0.0, jnp.maximum(cx, 0.0))
+        to_west = jnp.where(row == 0, 0.0, jnp.minimum(pltpu.roll(cx, 1, 0), 0.0))
         to_north = jnp.maximum(cy_n, 0.0)
         to_south = jnp.minimum(cy_s, 0.0)
         for tracer in range(TRACERS):
             n = tracer * LEV_DEV + lev
             a = adj[n]
-            a_east = jnp.where(row == LON - 1, east[n : n + 1, :], pltpu.roll(a, LON - 1, 0))
-            a_west = jnp.where(row == 0, west[n : n + 1, :], pltpu.roll(a, 1, 0))
-            a_north = pltpu.roll(a, LAT - 1, 1)
-            a_south = pltpu.roll(a, 1, 1)
             out[n] = (
                 a
-                + to_east * (a_east - a)
-                - to_west * (a_west - a)
-                + to_north * (a_north - a)
-                - to_south * (a_south - a)
+                + to_east * (pltpu.roll(a, LON - 1, 0) - a)
+                - to_west * (pltpu.roll(a, 1, 0) - a)
+                + to_north * (pltpu.roll(a, LAT - 1, 1) - a)
+                - to_south * (pltpu.roll(a, 1, 1) - a)
             )
 
 
@@ -138,9 +130,9 @@
     return [array[8 * (w // 2) : 8 * (w // 2) + 8, 128 * (w % 2) : 128 * (w % 2) + 128] for w in range(LEVS)]
 
 
-def force_body(received, advected, carry, ports, inner, blocks):
-    data = jnp.concatenate([received[:, 0, 128 * k : 128 * (k + 1)] for k in range(4)], 0)
-    where = received[:, 0, 512:640]
+def force_body(received, advected, forced):
+    data = jnp.concatenate([received[pl.ds(k, TILES, stride=5), :] for k in range(4)], 0)
+    where = received[pl.ds(4, TILES, stride=5), :]
     where = jnp.concatenate([where] + [pltpu.roll(where, 128 - 8 * k, 1) for k in range(1, 4)], 0)
     rows_all, lons = data.T, where.T
     lon_id = lax.broadcasted_iota(jnp.int32, (LON, 4 * TILES), 0).astype(F32)
@@ -155,15 +147,29 @@
         for piece in (coarse, fine):
             spread = [jnp.where(here, piece[r : r + 1, :], 0.0).astype(jnp.bfloat16) for r in range(ROWS)]
             total += jnp.dot(jnp.concatenate(spread, 0), hot, preferred_element_type=F32)
+    for n in range(ROWS):
+        forced[n] = advected[n] + total[n * LON : (n + 1) * LON]
+
+
+def condense_body(place, forced, first, second, first_own, second_own, carry, ports, inner, blocks):
+    even = place[0] % 2 == 0
+    row = lax.broadcasted_iota(jnp.int32, (LON, LAT), 0)
+    west = jnp.where(even, second[...], first[...])
+    east = jnp.where(even, first[...], second[...])
+    low_own = jnp.where(even, second_own[...], first_own[...])
+    high_own = jnp.where(even, first_own[...], second_own[...])
     for tracer in range(TRACERS):
-        forced = []
+        full = []
         for lev in range(LEV_DEV):
-            n = tracer * LEV_DEV + lev
-            forced.append(advected[n] + total[n * LON : (n + 1) * LON])
-        low = forced[0]
+            n, cx = tracer * LEV_DEV + lev, ROWS + lev
+            from_west = -jnp.minimum(west[cx : cx + 1], 0.0) * (west[n : n + 1] - low_own[n : n + 1])
+            from_east = jnp.maximum(high_own[cx : cx + 1], 0.0) * (east[n : n + 1] - high_own[n : n + 1])
+            across = jnp.where(row == 0, from_west, jnp.where(row == LON - 1, from_east, 0.0))
+            full.append(forced[n] + across)
+        low = full[0]
         high = jnp.zeros((LON, LAT), F32)
         for lev in range(1, LEV_DEV):
-            middle = high + forced[lev]
+            middle = high + full[lev]
             low = low + carry[0, lev - 1] * middle
             high = carry[1, lev - 1] * middle
             inner[tracer, lev - 1] = carry[2, lev - 1] * middle
@@ -204,16 +210,22 @@
                 ends[p, TRACERS + t] = zero
 
 
-def solve_body(inner, ends, carry, out):
+def solve_body(inner, ends, carry, out, result, sems):
     def whole(n):
         return jnp.concatenate([jnp.concatenate([ends[2 * a, n], ends[2 * a + 1, n]], 1) for a in range(4)], 0)
 
+    copies = []
     for tracer in range(TRACERS):
         bottom, level = whole(tracer), whole(TRACERS + tracer)
         for lev in range(LEV_DEV - 1, 0, -1):
             level = inner[tracer, lev - 1] + carry[0, lev - 1] * bottom + carry[1, lev - 1] * level
-            out[tracer * LEV_DEV + lev] = level
-        out[tracer * LEV_DEV] = bottom
+            result[tracer * LEV_DEV + lev] = level
+        result[tracer * LEV_DEV] = bottom
+        mine = pl.ds(tracer * LEV_DEV, LEV_DEV)
+        copies.append(pltpu.make_async_copy(result.at[mine], out.at[mine], sems.at[tracer]))
+        copies[-1].start()
+    for copy in copies:
+        copy.wait()
 
 
 def per_device(adjoint, wind_x, wind_y, kz, forcing, mon_cols, mon_counts):
@@ -222,25 +234,21 @@
     field = adjoint.reshape(ROWS, LON, LAT)
     inside = (LEV_DEV - 1, LON, LAT)
 
-    payload, first, second = pack(tile, forcing, mon_cols, mon_counts, field, wind_x)
-    received = lax.all_to_all(payload, "tile", 0, 0, tiled=True)
-    first = lax.ppermute(first, "tile", [(i, i ^ 1) for i in range(TILES)])
-    second = lax.ppermute(second, "tile", [(i, (i + 1 if i % 2 else i - 1) % TILES) for i in range(TILES)])
+    payload, first_own, second_own = pack(tile, forcing, mon_cols, mon_counts, field, wind_x)
+    second = lax.ppermute(second_own, "tile", [(i, (i + 1 if i % 2 else i - 1) % TILES) for i in range(TILES)])
+    first = lax.ppermute(first_own, "tile", [(i, i ^ 1) for i in range(TILES)])
+    received = lax.all_to_all(payload.reshape(TILES, 1, 640), "tile", 0, 0, tiled=True).reshape(TILES * 5, 128)
     carry, ports = call(block_body, ((3,) + inside, (3, LON, LAT)), [SMEM, VMEM])(place, kz)
-    (advected,) = call(advect_body, ((ROWS, LON, LAT),), [SMEM] + [VMEM] * 5, moved=2 << 20)(
-        tile, field, wind_x, wind_y, first, second
-    )
-    inner, blocks = call(
-        force_body,
-        ((TRACERS,) + inside, (LEVS, 11, 8, 128)),
-        [VMEM] * 4,
-        limit=24 << 20,
-        moved=2 << 20,
-    )(received, advected, carry, ports)
+    (advected,) = call(advect_body, ((ROWS, LON, LAT),), [VMEM] * 3, moved=2 << 20)(field, wind_x, wind_y)
+    (forced,) = call(force_body, ((ROWS, LON, LAT),), [VMEM] * 2, limit=24 << 20, moved=2 << 20)(received, advected)
+    inner, blocks = call(condense_body, ((TRACERS,) + inside, (LEVS, 11, 8, 128)), [SMEM] + [VMEM] * 7)(
+        tile, forced, first, second, first_own, second_own, carry, ports
+    )
     arrived = lax.all_to_all(blocks, "lev", 0, 0, tiled=True)
     (ends,) = call(chain_body, ((LEVS, 2 * TRACERS, 8, 128),), [VMEM])(arrived)
     ends = lax.all_to_all(ends, "lev", 0, 0, tiled=True)
-    (updated,) = call(solve_body, ((ROWS, LON, LAT),), [VMEM] * 3)(inner, ends, carry)
+    scratch = [pltpu.VMEM((ROWS, LON, LAT), F32), pltpu.SemaphoreType.DMA((TRACERS,))]
+    (updated,) = call(solve_body, ((ROWS, LON, LAT),), [VMEM] * 3, scratch, out_spec=HBM)(inner, ends, carry)
     return updated.reshape(adjoint.shape)
 
 

time: 70.9 us -> 68.8 us (0.970)
  waiting for transfers between devices: 1.95 us -> 0.01 us
    ppermute x2, waiting for transfers between devices: 1.94 us -> 0.01 us  [the longest x1 0.01 us: per_device(): first = lax.ppermute(first_own, 'tile', [(i, i ^ 1) for i in range(TILES)])]
    pallas_call x4 -> x5, Pallas kernels: 4.91 us -> 4.96 us  [the longest x1 2.08 us: pack(): call(pack_body, ((TILES * 5, 128), edge, edge), [SMEM] + [HBM] * 5, scratch)]
  transfers between devices with their start and end apart: 3 -> 3, of which waited for: 1 -> 0; matrix products, arithmetic and copies ran while one was open for 0% -> 0% of each run, Pallas kernels for 1% -> 3%
where the time goes in v3:
time: 68.8 us; the launch traced here: 68.5 us
  starting transfers between devices  33.5 us (49%)
  blocking collectives  29.2 us (42%)
  Pallas kernels  5.09 us (7%)
    all_to_all x1, starting transfers between devices, per_device(): lax.all_to_all(payload.reshape(TILES, 1, 640), 'tile', 0, 0, tiled=True)  19.7 us
    all_to_all x1, blocking collectives, per_device(): arrived = lax.all_to_all(blocks, 'lev', 0, 0, tiled=True)  17.3 us
    all_to_all x1, blocking collectives, per_device(): ends = lax.all_to_all(ends, 'lev', 0, 0, tiled=True)  11.9 us
    ppermute x1, starting transfers between devices, per_device(): lax.ppermute(second_own, 'tile', [(i, (i + 1 if i % 2 else i - 1) % TILES...  10.9 us
    ppermute x1, starting transfers between devices, per_device(): first = lax.ppermute(first_own, 'tile', [(i, i ^ 1) for i in range(TILES)])  2.92 us
    pallas_call x1, Pallas kernels, pack(): call(pack_body, ((TILES * 5, 128), edge, edge), [SMEM] + [HBM] * 5, scratch)  2.08 us
    pallas_call x1, Pallas kernels, per_device(): call(force_body, ((ROWS, LON, LAT),), [VMEM] * 2, limit=24 << 20, moved=2...  1.49 us
  transfers between devices with their start and end apart: 3, of which 0 were waited for; matrix products, arithmetic and copies ran while one was open for 0% of the time, Pallas kernels for 3%

profile of v3, /device:TPU:1, one launch (start us, length us, event | category | flops | bytes accessed | tf_op | source)
XLA Modules:
  0.0 68.5 jit_solution(9387737891715817500)
XLA Ops:
  0.0 0.0 copy-start
  0.0 2.1 %shard_map.73 = (f32[320,128]{1,0:T(8,128)}, f32[20,256]{1,0:T(8,128)S(1)}, f32[20,256]{1,0:T(8,128)S(1)}) custom-call(s32[1]{0:T(128)} %bitcast.place, f32[512,64]{1,0:T(8,128)} %bitcast.17, s32[32,64]{1,0:T(8,128)} %bitcast.18, s32[1,64]{1,0:T(1,128)} %counts.1, f32[16,32,256]{2,1,0:T(8,128)} %bitcast.14, f32[4,32,256]{2,1,0:T(8,128)} %wind_x.1), custom_call_target="tpu_custom_call" | custom-call | bytes 1048576 | tf_op jit(solution)/shard_map/pallas_call | solution.py:81
  2.1 0.0 copy-start.1
  2.1 0.0 copy-start.2
  2.1 19.7 %all-to-all-start = ((f32[64,1,640]{2,1,0:T(1,128)}), f32[64,1,640]{2,1,0:T(1,128)S(1)}, u32[]{:S(2)}, u32[]{:S(2)}) async-start(f32[64,1,640]{2,1,0:T(1,128)} %bitcast.7), calls=%async_computation | async-start | bytes 327680 | tf_op jit(solution)/shard_map/all_to_all | solution.py:240
  21.8 2.9 %collective-permute-start = (f32[20,256]{1,0:T(8,128)S(1)}, f32[20,256]{1,0:T(8,128)S(1)}, u32[]{:S(2)}, u32[]{:S(2)}) collective-permute-start(f32[20,256]{1,0:T(8,128)S(1)} %get-tuple-element.13.first_own), channel_id=1, source_target_pairs={{0,8},{8,0},{16,24},{24,16},{32,40},{40,32},{48,56},{56,48},{64,72... | collective-permute-start | bytes 61448 | tf_op jit(solution)/shard_map/ppermute | solution.py:239
  24.8 10.9 %collective-permute-start.1 = (f32[20,256]{1,0:T(8,128)S(1)}, f32[20,256]{1,0:T(8,128)S(1)}, u32[]{:S(2)}, u32[]{:S(2)}) collective-permute-start(f32[20,256]{1,0:T(8,128)S(1)} %get-tuple-element.14.second_own), channel_id=1, source_target_pairs={{0,504},{8,16},{16,8},{24,32},{32,24},{40,48},{48,40},{56,64},{64,... | collective-permute-start | bytes 61448 | tf_op jit(solution)/shard_map/ppermute | solution.py:238
  35.7 0.0 copy-done
  35.7 0.0 copy-done.1
  35.7 0.0 copy-done.2
  35.7 0.0 copy-start.3
  35.7 0.4 shard_map.74.advected
  36.2 0.5 copy-done.3
  36.7 0.0 all-to-all-done
  36.7 1.5 %shard_map.75.forced = f32[16,32,256]{2,1,0:T(8,128)S(1)} custom-call(f32[320,128]{1,0:T(8,128)S(1)} %bitcast.16, f32[16,32,256]{2,1,0:T(8,128)S(1)} %shard_map.74.advected), custom_call_target="tpu_custom_call" | custom-call | bytes 2097152 | tf_op jit(solution)/shard_map/pallas_call | solution.py:243
  38.2 0.0 collective-permute-done.first
  38.2 0.0 collective-permute-done.1.second
  38.2 0.1 shard_map.77
  38.3 17.3 %all_to_all.15.blocks = f32[8,11,8,128]{3,2,1,0:T(8,128)S(1)} all-to-all(f32[8,11,8,128]{3,2,1,0:T(8,128)S(1)} %get-tuple-element.18), channel_id=1, replica_groups=mesh['tile'=64,'lev'=8] {'lev'}, dimensions={0} | all-to-all | bytes 720896 | tf_op jit(solution)/shard_map/all_to_all | solution.py:247
  55.6 0.1 shard_map.78
  55.7 11.9 %all_to_all.16.ends = f32[8,8,8,128]{3,2,1,0:T(8,128)S(1)} all-to-all(f32[8,8,8,128]{3,2,1,0:T(8,128)S(1)} %shard_map.78), channel_id=1, replica_groups=mesh['tile'=64,'lev'=8] {'lev'}, dimensions={0} | all-to-all | bytes 524288 | tf_op jit(solution)/shard_map/all_to_all | solution.py:249
  67.7 0.8 %shard_map.79 = f32[16,32,256]{2,1,0:T(8,128)} custom-call(f32[4,3,32,256]{3,2,1,0:T(8,128)S(1)} %get-tuple-element.17.inner, f32[8,8,8,128]{3,2,1,0:T(8,128)S(1)} %all_to_all.16.ends, f32[3,3,32,256]{3,2,1,0:T(8,128)S(1)} %get-tuple-element.15.carry), custom_call_target="tpu_custom_call" | custom-call | bytes 1048576 | tf_op jit(solution)/shard_map/pallas_call | solution.py:251
  (1 shorter events, 0.0 us)
Async XLA Ops:
  0.0 35.7 %copy-start = (f32[4,4,32,256]{3,2,1,0:T(8,128)S(1)}, f32[4,4,32,256]{3,2,1,0:T(8,128)}, u32[]{:S(2)}) copy-start(f32[4,4,32,256]{3,2,1,0:T(8,128)} %param.7) | copy-start | bytes 1572868
  2.1 33.6 %copy-start.1 = (f32[4,32,256]{2,1,0:T(8,128)S(1)}, f32[4,32,256]{2,1,0:T(8,128)}, u32[]{:S(2)}) copy-start(f32[4,32,256]{2,1,0:T(8,128)} %wind_x.1) | copy-start | bytes 393220
  2.1 33.6 %copy-start.2 = (f32[4,32,256]{2,1,0:T(8,128)S(1)}, f32[4,32,256]{2,1,0:T(8,128)}, u32[]{:S(2)}) copy-start(f32[4,32,256]{2,1,0:T(8,128)} %wind_y.1) | copy-start | bytes 393220
  2.1 34.6 %all-to-all-start = ((f32[64,1,640]{2,1,0:T(1,128)}), f32[64,1,640]{2,1,0:T(1,128)S(1)}, u32[]{:S(2)}, u32[]{:S(2)}) async-start(f32[64,1,640]{2,1,0:T(1,128)} %bitcast.7), calls=%async_computation | async-start | bytes 327680 | tf_op jit(solution)/shard_map/all_to_all | solution.py:240
  21.8 16.4 %collective-permute-start = (f32[20,256]{1,0:T(8,128)S(1)}, f32[20,256]{1,0:T(8,128)S(1)}, u32[]{:S(2)}, u32[]{:S(2)}) collective-permute-start(f32[20,256]{1,0:T(8,128)S(1)} %get-tuple-element.13.first_own), channel_id=1, source_target_pairs={{0,8},{8,0},{16,24},{24,16},{32,40},{40,32},{48,56},{56,48},{64,72... | collective-permute-start | bytes 61448 | tf_op jit(solution)/shard_map/ppermute | solution.py:239
  24.8 13.4 %collective-permute-start.1 = (f32[20,256]{1,0:T(8,128)S(1)}, f32[20,256]{1,0:T(8,128)S(1)}, u32[]{:S(2)}, u32[]{:S(2)}) collective-permute-start(f32[20,256]{1,0:T(8,128)S(1)} %get-tuple-element.14.second_own), channel_id=1, source_target_pairs={{0,504},{8,16},{16,8},{24,32},{32,24},{40,48},{48,40},{56,64},{64,... | collective-permute-start | bytes 61448 | tf_op jit(solution)/shard_map/ppermute | solution.py:238
  35.7 0.9 %copy-start.3 = (f32[4,32,256]{2,1,0:T(8,128)S(1)}, f32[4,32,256]{2,1,0:T(8,128)}, u32[]{:S(2)}) copy-start(f32[4,32,256]{2,1,0:T(8,128)} %kz.1) | copy-start | bytes 393220

commit v4 on v3

--- a/solution.py
+++ b/solution.py
@@ -27,7 +27,7 @@
         body,
         out_shape=shapes,
         in_specs=in_specs,
-        out_specs=tuple(out_spec for _ in outs),
+        out_specs=out_spec if isinstance(out_spec, tuple) else (out_spec,) * len(outs),
         scratch_shapes=list(scratch),
         compiler_params=pltpu.CompilerParams(vmem_limit_bytes=limit),
         cost_estimate=pl.CostEstimate(flops=flops, bytes_accessed=moved, transcendentals=0),
@@ -35,7 +35,7 @@
     )
 
 
-def pack_body(place, force, cols, counts, adj, wind, payload, first, second, force_v, cols_v, counts_v, low_v, high_v, wind_v, sems):
+def pack_body(place, force, cols, counts, adj, wind, payload, first, second, force_v, cols_v, counts_v, low_v, high_v, wind_v, message, sems):
     last = pl.ds(LON - 8, 8)
     copies = [
         pltpu.make_async_copy(force, force_v, sems.at[0]),
@@ -47,21 +47,26 @@
     ]
     for copy in copies:
         copy.start()
-    for copy in copies:
+    for copy in copies[:3]:
         copy.wait()
     for k in range(4):
         parts = [force_v[pl.ds(8 * k + g, ROWS, stride=CAP), :] for g in range(8)]
-        payload[pl.ds(k, TILES, stride=5), :] = jnp.concatenate(parts, 0).T
+        message[pl.ds(k, TILES, stride=5), :] = jnp.concatenate(parts, 0).T
     slot = lax.broadcasted_iota(jnp.int32, (CAP, TILES), 0)
     lon = jnp.where(slot < counts_v[...], cols_v[...] >> 8, -1).astype(F32)
     lat = (cols_v[...] & 255).astype(F32)
-    payload[pl.ds(4, TILES, stride=5), :] = jnp.concatenate([lon, lat, jnp.zeros((64, TILES), F32)], 0).T
+    message[pl.ds(4, TILES, stride=5), :] = jnp.concatenate([lon, lat, jnp.zeros((64, TILES), F32)], 0).T
+    out = pltpu.make_async_copy(message, payload, sems.at[6])
+    out.start()
+    for copy in copies[3:]:
+        copy.wait()
     even = place[0] % 2 == 0
     low, high, cx = low_v[:, 0, :], high_v[:, 7, :], wind_v[:, 7, :]
     first[0:ROWS, :] = jnp.where(even, high, low)
     second[0:ROWS, :] = jnp.where(even, low, high)
     first[ROWS : ROWS + LEV_DEV, :] = cx
     second[ROWS : ROWS + LEV_DEV, :] = cx
+    out.wait()
 
 
 def pack(tile, forcing, mon_cols, mon_counts, field, wind_x):
@@ -75,13 +80,14 @@
         pltpu.VMEM((ROWS, 8, LAT), F32),
         pltpu.VMEM((ROWS, 8, LAT), F32),
         pltpu.VMEM((LEV_DEV, 8, LAT), F32),
-        pltpu.SemaphoreType.DMA((6,)),
+        pltpu.VMEM((TILES * 5, 128), F32),
+        pltpu.SemaphoreType.DMA((7,)),
     ]
     operands = [pltpu.with_memory_space_constraint(x, pltpu.HBM) for x in (force, cols, mon_counts, field, wind_x)]
-    return call(pack_body, ((TILES * 5, 128), edge, edge), [SMEM] + [HBM] * 5, scratch)(tile, *operands)
-
-
-def advect_body(adj, wind_x, wind_y, out):
+    return call(pack_body, ((TILES * 5, 128), edge, edge), [SMEM] + [HBM] * 5, scratch, out_spec=(HBM, VMEM, VMEM))(tile, *operands)
+
+
+def prepare_body(place, adj, wind_x, wind_y, kz, out, carry, ports):
     row = lax.broadcasted_iota(jnp.int32, (LON, LAT), 0)
     lane = lax.broadcasted_iota(jnp.int32, (LON, LAT), 1)
     for lev in range(LEV_DEV):
@@ -102,9 +108,6 @@
                 + to_north * (pltpu.roll(a, LAT - 1, 1) - a)
                 - to_south * (pltpu.roll(a, 1, 1) - a)
             )
-
-
-def block_body(place, kz, carry, ports):
     shunt = jnp.ones((LON, LAT), F32)
     series = kz[0]
     top = jnp.zeros((LON, LAT), F32)
@@ -238,8 +241,12 @@
     second = lax.ppermute(second_own, "tile", [(i, (i + 1 if i % 2 else i - 1) % TILES) for i in range(TILES)])
     first = lax.ppermute(first_own, "tile", [(i, i ^ 1) for i in range(TILES)])
     received = lax.all_to_all(payload.reshape(TILES, 1, 640), "tile", 0, 0, tiled=True).reshape(TILES * 5, 128)
-    carry, ports = call(block_body, ((3,) + inside, (3, LON, LAT)), [SMEM, VMEM])(place, kz)
-    (advected,) = call(advect_body, ((ROWS, LON, LAT),), [VMEM] * 3, moved=2 << 20)(field, wind_x, wind_y)
+    advected, carry, ports = call(
+        prepare_body,
+        ((ROWS, LON, LAT), (3,) + inside, (3, LON, LAT)),
+        [SMEM] + [VMEM] * 4,
+        moved=2 << 20,
+    )(place, field, wind_x, wind_y, kz)
     (forced,) = call(force_body, ((ROWS, LON, LAT),), [VMEM] * 2, limit=24 << 20, moved=2 << 20)(received, advected)
     inner, blocks = call(condense_body, ((TRACERS,) + inside, (LEVS, 11, 8, 128)), [SMEM] + [VMEM] * 7)(
         tile, forced, first, second, first_own, second_own, carry, ports

time: 68.8 us -> 68.7 us (level)
    pallas_call x3 -> x2, Pallas kernels: 2.54 us -> 2.41 us  [the longest x1 1.95 us: pack(): call(pack_body, ((TILES * 5, 128), edge, edge), [SMEM] + [HBM] * 5, scrat...]
  transfers between devices with their start and end apart: 3 -> 3, of which waited for: 0 -> 1; matrix products, arithmetic and copies ran while one was open for 0% -> 0% of each run, Pallas kernels for 3% -> 3%
where the time goes in v4:
time: 68.7 us; the launch traced here: 68.4 us
  starting transfers between devices  33.5 us (49%)
  blocking collectives  29.7 us (43%)
  Pallas kernels  4.95 us (7%)
    all_to_all x1, starting transfers between devices, per_device(): lax.all_to_all(payload.reshape(TILES, 1, 640), 'tile', 0, 0, tiled=True)  19.7 us
    all_to_all x1, blocking collectives, per_device(): arrived = lax.all_to_all(blocks, 'lev', 0, 0, tiled=True)  17.8 us
    all_to_all x1, blocking collectives, per_device(): ends = lax.all_to_all(ends, 'lev', 0, 0, tiled=True)  11.9 us
    ppermute x1, starting transfers between devices, per_device(): lax.ppermute(second_own, 'tile', [(i, (i + 1 if i % 2 else i - 1) % TILES...  10.9 us
    ppermute x1, starting transfers between devices, per_device(): first = lax.ppermute(first_own, 'tile', [(i, i ^ 1) for i in range(TILES)])  2.92 us
    pallas_call x1, Pallas kernels, pack(): call(pack_body, ((TILES * 5, 128), edge, edge), [SMEM] + [HBM] * 5, scrat...  1.95 us
    pallas_call x1, Pallas kernels, per_device(): call(force_body, ((ROWS, LON, LAT),), [VMEM] * 2, limit=24 << 20, moved=2...  1.49 us
  transfers between devices with their start and end apart: 3, of which 1 were waited for; matrix products, arithmetic and copies ran while one was open for 0% of the time, Pallas kernels for 3%

profile of v4, /device:TPU:1, one launch (start us, length us, event | category | flops | bytes accessed | tf_op | source)
XLA Modules:
  0.0 68.4 jit_solution(17827083698419645287)
XLA Ops:
  0.0 0.0 copy-start
  0.0 0.0 copy-start.3
  0.0 2.0 %shard_map.73 = (f32[320,128]{1,0:T(8,128)}, f32[20,256]{1,0:T(8,128)S(1)}, f32[20,256]{1,0:T(8,128)S(1)}) custom-call(s32[1]{0:T(128)} %bitcast.place, f32[512,64]{1,0:T(8,128)} %bitcast.17, s32[32,64]{1,0:T(8,128)} %bitcast.18, s32[1,64]{1,0:T(1,128)} %counts.1, f32[16,32,256]{2,1,0:T(8,128)} %bitcast.14, f32[4,32,256]{2,1,0:T(8,128)} %wind_x.1), custom_call_target="tpu_custom_call" | custom-call | bytes 1048576 | tf_op jit(solution)/shard_map/pallas_call | solution.py:87
  2.0 0.0 copy-start.1
  2.0 0.0 copy-start.2
  2.0 19.7 %all-to-all-start = ((f32[64,1,640]{2,1,0:T(1,128)}), f32[64,1,640]{2,1,0:T(1,128)S(1)}, u32[]{:S(2)}, u32[]{:S(2)}) async-start(f32[64,1,640]{2,1,0:T(1,128)} %bitcast.7), calls=%async_computation | async-start | bytes 327680 | tf_op jit(solution)/shard_map/all_to_all | solution.py:243
  21.7 2.9 %collective-permute-start = (f32[20,256]{1,0:T(8,128)S(1)}, f32[20,256]{1,0:T(8,128)S(1)}, u32[]{:S(2)}, u32[]{:S(2)}) collective-permute-start(f32[20,256]{1,0:T(8,128)S(1)} %get-tuple-element.15.first_own), channel_id=1, source_target_pairs={{0,8},{8,0},{16,24},{24,16},{32,40},{40,32},{48,56},{56,48},{64,72... | collective-permute-start | bytes 61448 | tf_op jit(solution)/shard_map/ppermute | solution.py:242
  24.6 10.9 %collective-permute-start.1 = (f32[20,256]{1,0:T(8,128)S(1)}, f32[20,256]{1,0:T(8,128)S(1)}, u32[]{:S(2)}, u32[]{:S(2)}) collective-permute-start(f32[20,256]{1,0:T(8,128)S(1)} %get-tuple-element.16.second_own), channel_id=1, source_target_pairs={{0,504},{8,16},{16,8},{24,32},{32,24},{40,48},{48,40},{56,64},{64,... | collective-permute-start | bytes 61448 | tf_op jit(solution)/shard_map/ppermute | solution.py:241
  35.6 0.0 copy-done
  35.6 0.0 copy-done.3
  35.6 0.0 copy-done.1
  35.6 0.0 copy-done.2
  35.6 0.5 shard_map.74
  36.1 0.0 all-to-all-done
  36.1 1.5 %shard_map.75.forced = f32[16,32,256]{2,1,0:T(8,128)S(1)} custom-call(f32[320,128]{1,0:T(8,128)S(1)} %bitcast.16, f32[16,32,256]{2,1,0:T(8,128)S(1)} %get-tuple-element.14.advected), custom_call_target="tpu_custom_call" | custom-call | bytes 2097152 | tf_op jit(solution)/shard_map/pallas_call | solution.py:250
  37.6 0.0 collective-permute-done.first
  37.6 0.1 collective-permute-done.1.second
  37.6 0.1 shard_map.76
  37.8 17.8 %all_to_all.15.blocks = f32[8,11,8,128]{3,2,1,0:T(8,128)S(1)} all-to-all(f32[8,11,8,128]{3,2,1,0:T(8,128)S(1)} %get-tuple-element.20), channel_id=1, replica_groups=mesh['tile'=64,'lev'=8] {'lev'}, dimensions={0} | all-to-all | bytes 720896 | tf_op jit(solution)/shard_map/all_to_all | solution.py:254
  55.5 0.1 shard_map.77
  55.6 11.9 %all_to_all.16.ends = f32[8,8,8,128]{3,2,1,0:T(8,128)S(1)} all-to-all(f32[8,8,8,128]{3,2,1,0:T(8,128)S(1)} %shard_map.77), channel_id=1, replica_groups=mesh['tile'=64,'lev'=8] {'lev'}, dimensions={0} | all-to-all | bytes 524288 | tf_op jit(solution)/shard_map/all_to_all | solution.py:256
  67.5 0.8 %shard_map.78 = f32[16,32,256]{2,1,0:T(8,128)} custom-call(f32[4,3,32,256]{3,2,1,0:T(8,128)S(1)} %get-tuple-element.19.inner, f32[8,8,8,128]{3,2,1,0:T(8,128)S(1)} %all_to_all.16.ends, f32[3,3,32,256]{3,2,1,0:T(8,128)S(1)} %get-tuple-element.17.carry), custom_call_target="tpu_custom_call" | custom-call | bytes 1048576 | tf_op jit(solution)/shard_map/pallas_call | solution.py:258
Async XLA Ops:
  0.0 35.6 %copy-start = (f32[4,4,32,256]{3,2,1,0:T(8,128)S(1)}, f32[4,4,32,256]{3,2,1,0:T(8,128)}, u32[]{:S(2)}) copy-start(f32[4,4,32,256]{3,2,1,0:T(8,128)} %param.7) | copy-start | bytes 1572868
  0.0 35.6 %copy-start.3 = (f32[4,32,256]{2,1,0:T(8,128)S(1)}, f32[4,32,256]{2,1,0:T(8,128)}, u32[]{:S(2)}) copy-start(f32[4,32,256]{2,1,0:T(8,128)} %kz.1) | copy-start | bytes 393220
  2.0 33.6 %copy-start.1 = (f32[4,32,256]{2,1,0:T(8,128)S(1)}, f32[4,32,256]{2,1,0:T(8,128)}, u32[]{:S(2)}) copy-start(f32[4,32,256]{2,1,0:T(8,128)} %wind_x.1) | copy-start | bytes 393220
  2.0 33.6 %copy-start.2 = (f32[4,32,256]{2,1,0:T(8,128)S(1)}, f32[4,32,256]{2,1,0:T(8,128)}, u32[]{:S(2)}) copy-start(f32[4,32,256]{2,1,0:T(8,128)} %wind_y.1) | copy-start | bytes 393220
  2.0 34.1 %all-to-all-start = ((f32[64,1,640]{2,1,0:T(1,128)}), f32[64,1,640]{2,1,0:T(1,128)S(1)}, u32[]{:S(2)}, u32[]{:S(2)}) async-start(f32[64,1,640]{2,1,0:T(1,128)} %bitcast.7), calls=%async_computation | async-start | bytes 327680 | tf_op jit(solution)/shard_map/all_to_all | solution.py:243
  21.7 15.9 %collective-permute-start = (f32[20,256]{1,0:T(8,128)S(1)}, f32[20,256]{1,0:T(8,128)S(1)}, u32[]{:S(2)}, u32[]{:S(2)}) collective-permute-start(f32[20,256]{1,0:T(8,128)S(1)} %get-tuple-element.15.first_own), channel_id=1, source_target_pairs={{0,8},{8,0},{16,24},{24,16},{32,40},{40,32},{48,56},{56,48},{64,72... | collective-permute-start | bytes 61448 | tf_op jit(solution)/shard_map/ppermute | solution.py:242
  24.6 13.0 %collective-permute-start.1 = (f32[20,256]{1,0:T(8,128)S(1)}, f32[20,256]{1,0:T(8,128)S(1)}, u32[]{:S(2)}, u32[]{:S(2)}) collective-permute-start(f32[20,256]{1,0:T(8,128)S(1)} %get-tuple-element.16.second_own), channel_id=1, source_target_pairs={{0,504},{8,16},{16,8},{24,32},{32,24},{40,48},{48,40},{56,64},{64,... | collective-permute-start | bytes 61448 | tf_op jit(solution)/shard_map/ppermute | solution.py:241

commit v5 on v4

--- a/solution.py
+++ b/solution.py
@@ -35,15 +35,18 @@
     )
 
 
-def pack_body(place, force, cols, counts, adj, wind, payload, first, second, force_v, cols_v, counts_v, low_v, high_v, wind_v, message, sems):
-    last = pl.ds(LON - 8, 8)
+def pack_body(
+    tile, place, force, cols, counts, adj, wind, wind_y, kz, payload, first, second, advected, carry, ports,
+    force_v, cols_v, counts_v, adj_v, wind_v, wind_y_v, kz_v, message, sems,
+):
     copies = [
         pltpu.make_async_copy(force, force_v, sems.at[0]),
         pltpu.make_async_copy(cols, cols_v, sems.at[1]),
         pltpu.make_async_copy(counts, counts_v, sems.at[2]),
-        pltpu.make_async_copy(adj.at[:, pl.ds(0, 8), :], low_v, sems.at[3]),
-        pltpu.make_async_copy(adj.at[:, last, :], high_v, sems.at[4]),
-        pltpu.make_async_copy(wind.at[:, last, :], wind_v, sems.at[5]),
+        pltpu.make_async_copy(adj, adj_v, sems.at[3]),
+        pltpu.make_async_copy(wind, wind_v, sems.at[4]),
+        pltpu.make_async_copy(wind_y, wind_y_v, sems.at[5]),
+        pltpu.make_async_copy(kz, kz_v, sems.at[7]),
     ]
     for copy in copies:
         copy.start()
@@ -60,16 +63,17 @@
     out.start()
     for copy in copies[3:]:
         copy.wait()
-    even = place[0] % 2 == 0
-    low, high, cx = low_v[:, 0, :], high_v[:, 7, :], wind_v[:, 7, :]
+    even = tile[0] % 2 == 0
+    low, high, cx = adj_v[:, 0, :], adj_v[:, LON - 1, :], wind_v[:, LON - 1, :]
     first[0:ROWS, :] = jnp.where(even, high, low)
     second[0:ROWS, :] = jnp.where(even, low, high)
     first[ROWS : ROWS + LEV_DEV, :] = cx
     second[ROWS : ROWS + LEV_DEV, :] = cx
+    prepare_body(place, adj_v, wind_v, wind_y_v, kz_v, advected, carry, ports)
     out.wait()
 
 
-def pack(tile, forcing, mon_cols, mon_counts, field, wind_x):
+def pack(tile, place, forcing, mon_cols, mon_counts, field, wind_x, wind_y, kz):
     force = jnp.transpose(forcing[0], (1, 2, 3, 0)).reshape(ROWS * CAP, TILES)
     cols = jnp.transpose(mon_cols[0], (1, 0))
     edge = (ROWS + LEV_DEV, LAT)
@@ -77,14 +81,17 @@
         pltpu.VMEM((ROWS * CAP, TILES), F32),
         pltpu.VMEM((CAP, TILES), jnp.int32),
         pltpu.VMEM((1, TILES), jnp.int32),
-        pltpu.VMEM((ROWS, 8, LAT), F32),
-        pltpu.VMEM((ROWS, 8, LAT), F32),
-        pltpu.VMEM((LEV_DEV, 8, LAT), F32),
+        pltpu.VMEM((ROWS, LON, LAT), F32),
+        pltpu.VMEM((LEV_DEV, LON, LAT), F32),
+        pltpu.VMEM((LEV_DEV, LON, LAT), F32),
+        pltpu.VMEM((LEV_DEV, LON, LAT), F32),
         pltpu.VMEM((TILES * 5, 128), F32),
-        pltpu.SemaphoreType.DMA((7,)),
+        pltpu.SemaphoreType.DMA((8,)),
     ]
-    operands = [pltpu.with_memory_space_constraint(x, pltpu.HBM) for x in (force, cols, mon_counts, field, wind_x)]
-    return call(pack_body, ((TILES * 5, 128), edge, edge), [SMEM] + [HBM] * 5, scratch, out_spec=(HBM, VMEM, VMEM))(tile, *operands)
+    operands = [pltpu.with_memory_space_constraint(x, pltpu.HBM) for x in (force, cols, mon_counts, field, wind_x, wind_y, kz)]
+    outs = ((TILES * 5, 128), edge, edge, (ROWS, LON, LAT), (3, LEV_DEV - 1, LON, LAT), (3, LON, LAT))
+    specs = [SMEM] * 2 + [HBM] * 7
+    return call(pack_body, outs, specs, scratch, out_spec=(HBM,) + (VMEM,) * 5)(tile, place, *operands)
 
 
 def prepare_body(place, adj, wind_x, wind_y, kz, out, carry, ports):
@@ -237,16 +244,12 @@
     field = adjoint.reshape(ROWS, LON, LAT)
     inside = (LEV_DEV - 1, LON, LAT)
 
-    payload, first_own, second_own = pack(tile, forcing, mon_cols, mon_counts, field, wind_x)
+    payload, first_own, second_own, advected, carry, ports = pack(
+        tile, place, forcing, mon_cols, mon_counts, field, wind_x, wind_y, kz
+    )
     second = lax.ppermute(second_own, "tile", [(i, (i + 1 if i % 2 else i - 1) % TILES) for i in range(TILES)])
     first = lax.ppermute(first_own, "tile", [(i, i ^ 1) for i in range(TILES)])
     received = lax.all_to_all(payload.reshape(TILES, 1, 640), "tile", 0, 0, tiled=True).reshape(TILES * 5, 128)
-    advected, carry, ports = call(
-        prepare_body,
-        ((ROWS, LON, LAT), (3,) + inside, (3, LON, LAT)),
-        [SMEM] + [VMEM] * 4,
-        moved=2 << 20,
-    )(place, field, wind_x, wind_y, kz)
     (forced,) = call(force_body, ((ROWS, LON, LAT),), [VMEM] * 2, limit=24 << 20, moved=2 << 20)(received, advected)
     inner, blocks = call(condense_body, ((TRACERS,) + inside, (LEVS, 11, 8, 128)), [SMEM] + [VMEM] * 7)(
         tile, forced, first, second, first_own, second_own, carry, ports

time: 68.7 us -> 68.5 us (level)
    pallas_call x2 -> x1, Pallas kernels: 2.41 us -> 1.9 us  [pack(): call(pack_body, outs, specs, scratch, out_spec=(HBM,) + (VMEM,) * 5)]
  transfers between devices with their start and end apart: 3 -> 3, of which waited for: 1 -> 1; matrix products, arithmetic and copies ran while one was open for 0% -> 0% of each run, Pallas kernels for 3% -> 2%
where the time goes in v5:
time: 68.5 us; the launch traced here: 68.2 us
  starting transfers between devices  33.4 us (49%)
  blocking collectives  29.7 us (43%)
  Pallas kernels  4.44 us (6%)
    all_to_all x1, starting transfers between devices, per_device(): lax.all_to_all(payload.reshape(TILES, 1, 640), 'tile', 0, 0, tiled=True)  19.6 us
    all_to_all x1, blocking collectives, per_device(): arrived = lax.all_to_all(blocks, 'lev', 0, 0, tiled=True)  17.8 us
    all_to_all x1, blocking collectives, per_device(): ends = lax.all_to_all(ends, 'lev', 0, 0, tiled=True)  11.9 us
    ppermute x1, starting transfers between devices, per_device(): lax.ppermute(second_own, 'tile', [(i, (i + 1 if i % 2 else i - 1) % TILES...  10.9 us
    ppermute x1, starting transfers between devices, per_device(): first = lax.ppermute(first_own, 'tile', [(i, i ^ 1) for i in range(TILES)])  2.92 us
    pallas_call x1, Pallas kernels, pack(): call(pack_body, outs, specs, scratch, out_spec=(HBM,) + (VMEM,) * 5)  1.9 us
    pallas_call x1, Pallas kernels, per_device(): call(force_body, ((ROWS, LON, LAT),), [VMEM] * 2, limit=24 << 20, moved=2...  1.49 us
  transfers between devices with their start and end apart: 3, of which 1 were waited for; matrix products, arithmetic and copies ran while one was open for 0% of the time, Pallas kernels for 2%

profile of v5, /device:TPU:1, one launch (start us, length us, event | category | flops | bytes accessed | tf_op | source)
XLA Modules:
  0.0 68.2 jit_solution(13338304774971786273)
XLA Ops:
  0.0 1.9 %shard_map.73 = (f32[320,128]{1,0:T(8,128)}, f32[20,256]{1,0:T(8,128)S(1)}, f32[20,256]{1,0:T(8,128)S(1)}, f32[16,32,256]{2,1,0:T(8,128)S(1)}, f32[3,3,32,256]{3,2,1,0:T(8,128)S(1)}, /*index=5*/f32[3,32,256]{2,1,0:T(8,128)S(1)}) custom-call(s32[1]{0:T(128)} %bitcast.tile.place, s32[1]{0:T(128)} %bitcast.1.place, f32[512,64]{1,0:T(8,128)} %bitcast.16, ...), custom_call_target="tpu_custom_call" | custom-call | bytes 1048576 | tf_op jit(solution)/shard_map/pallas_call | solution.py:94
  1.9 19.6 %all-to-all-start = ((f32[64,1,640]{2,1,0:T(1,128)}), f32[64,1,640]{2,1,0:T(1,128)S(1)}, u32[]{:S(2)}, u32[]{:S(2)}) async-start(f32[64,1,640]{2,1,0:T(1,128)} %bitcast.8), calls=%async_computation | async-start | bytes 327680 | tf_op jit(solution)/shard_map/all_to_all | solution.py:252
  21.5 2.9 %collective-permute-start = (f32[20,256]{1,0:T(8,128)S(1)}, f32[20,256]{1,0:T(8,128)S(1)}, u32[]{:S(2)}, u32[]{:S(2)}) collective-permute-start(f32[20,256]{1,0:T(8,128)S(1)} %get-tuple-element.15.first_own), channel_id=1, source_target_pairs={{0,8},{8,0},{16,24},{24,16},{32,40},{40,32},{48,56},{56,48},{64,72... | collective-permute-start | bytes 61448 | tf_op jit(solution)/shard_map/ppermute | solution.py:251
  24.4 10.9 %collective-permute-start.1 = (f32[20,256]{1,0:T(8,128)S(1)}, f32[20,256]{1,0:T(8,128)S(1)}, u32[]{:S(2)}, u32[]{:S(2)}) collective-permute-start(f32[20,256]{1,0:T(8,128)S(1)} %get-tuple-element.16.second_own), channel_id=1, source_target_pairs={{0,504},{8,16},{16,8},{24,32},{32,24},{40,48},{48,40},{56,64},{64,... | collective-permute-start | bytes 61448 | tf_op jit(solution)/shard_map/ppermute | solution.py:250
  35.3 0.0 all-to-all-done
  35.4 1.5 %shard_map.74.forced = f32[16,32,256]{2,1,0:T(8,128)S(1)} custom-call(f32[320,128]{1,0:T(8,128)S(1)} %bitcast.14, f32[16,32,256]{2,1,0:T(8,128)S(1)} %get-tuple-element.14.advected), custom_call_target="tpu_custom_call" | custom-call | bytes 2097152 | tf_op jit(solution)/shard_map/pallas_call | solution.py:253
  36.9 0.0 collective-permute-done.first
  36.9 0.6 collective-permute-done.1.second
  37.4 0.1 shard_map.75
  37.5 17.8 %all_to_all.15.blocks = f32[8,11,8,128]{3,2,1,0:T(8,128)S(1)} all-to-all(f32[8,11,8,128]{3,2,1,0:T(8,128)S(1)} %get-tuple-element.20), channel_id=1, replica_groups=mesh['tile'=64,'lev'=8] {'lev'}, dimensions={0} | all-to-all | bytes 720896 | tf_op jit(solution)/shard_map/all_to_all | solution.py:257
  55.3 0.1 shard_map.76
  55.4 11.9 %all_to_all.16.ends = f32[8,8,8,128]{3,2,1,0:T(8,128)S(1)} all-to-all(f32[8,8,8,128]{3,2,1,0:T(8,128)S(1)} %shard_map.76), channel_id=1, replica_groups=mesh['tile'=64,'lev'=8] {'lev'}, dimensions={0} | all-to-all | bytes 524288 | tf_op jit(solution)/shard_map/all_to_all | solution.py:259
  67.3 0.8 %shard_map.77 = f32[16,32,256]{2,1,0:T(8,128)} custom-call(f32[4,3,32,256]{3,2,1,0:T(8,128)S(1)} %get-tuple-element.19.inner, f32[8,8,8,128]{3,2,1,0:T(8,128)S(1)} %all_to_all.16.ends, f32[3,3,32,256]{3,2,1,0:T(8,128)S(1)} %get-tuple-element.17.carry), custom_call_target="tpu_custom_call" | custom-call | bytes 1048576 | tf_op jit(solution)/shard_map/pallas_call | solution.py:261
Async XLA Ops:
  1.9 33.4 %all-to-all-start = ((f32[64,1,640]{2,1,0:T(1,128)}), f32[64,1,640]{2,1,0:T(1,128)S(1)}, u32[]{:S(2)}, u32[]{:S(2)}) async-start(f32[64,1,640]{2,1,0:T(1,128)} %bitcast.8), calls=%async_computation | async-start | bytes 327680 | tf_op jit(solution)/shard_map/all_to_all | solution.py:252
  21.5 15.4 %collective-permute-start = (f32[20,256]{1,0:T(8,128)S(1)}, f32[20,256]{1,0:T(8,128)S(1)}, u32[]{:S(2)}, u32[]{:S(2)}) collective-permute-start(f32[20,256]{1,0:T(8,128)S(1)} %get-tuple-element.15.first_own), channel_id=1, source_target_pairs={{0,8},{8,0},{16,24},{24,16},{32,40},{40,32},{48,56},{56,48},{64,72... | collective-permute-start | bytes 61448 | tf_op jit(solution)/shard_map/ppermute | solution.py:251
  24.4 13.0 %collective-permute-start.1 = (f32[20,256]{1,0:T(8,128)S(1)}, f32[20,256]{1,0:T(8,128)S(1)}, u32[]{:S(2)}, u32[]{:S(2)}) collective-permute-start(f32[20,256]{1,0:T(8,128)S(1)} %get-tuple-element.16.second_own), channel_id=1, source_target_pairs={{0,504},{8,16},{16,8},{24,32},{32,24},{40,48},{48,40},{56,64},{64,... | collective-permute-start | bytes 61448 | tf_op jit(solution)/shard_map/ppermute | solution.py:250

commit v6 on v5

--- a/solution.py
+++ b/solution.py
@@ -140,6 +140,10 @@
     return [array[8 * (w // 2) : 8 * (w // 2) + 8, 128 * (w % 2) : 128 * (w % 2) + 128] for w in range(LEVS)]
 
 
+def pass_body(near, out):
+    out[...] = near[...]
+
+
 def force_body(received, advected, forced):
     data = jnp.concatenate([received[pl.ds(k, TILES, stride=5), :] for k in range(4)], 0)
     where = received[pl.ds(4, TILES, stride=5), :]
@@ -248,7 +252,8 @@
         tile, place, forcing, mon_cols, mon_counts, field, wind_x, wind_y, kz
     )
     second = lax.ppermute(second_own, "tile", [(i, (i + 1 if i % 2 else i - 1) % TILES) for i in range(TILES)])
-    first = lax.ppermute(first_own, "tile", [(i, i ^ 1) for i in range(TILES)])
+    (near,) = call(pass_body, (first_own.shape,), [VMEM])(first_own)
+    first = lax.ppermute(near, "tile", [(i, i ^ 1) for i in range(TILES)])
     received = lax.all_to_all(payload.reshape(TILES, 1, 640), "tile", 0, 0, tiled=True).reshape(TILES * 5, 128)
     (forced,) = call(force_body, ((ROWS, LON, LAT),), [VMEM] * 2, limit=24 << 20, moved=2 << 20)(received, advected)
     inner, blocks = call(condense_body, ((TRACERS,) + inside, (LEVS, 11, 8, 128)), [SMEM] + [VMEM] * 7)(

time: 68.5 us -> 68.5 us (level)
  no operation moved by 1% of the time
where the time goes in v6:
time: 68.5 us; the launch traced here: 68.2 us
  starting transfers between devices  33.4 us (49%)
  blocking collectives  29.7 us (43%)
  Pallas kernels  4.44 us (6%)
    all_to_all x1, starting transfers between devices, per_device(): lax.all_to_all(payload.reshape(TILES, 1, 640), 'tile', 0, 0, tiled=True)  19.6 us
    all_to_all x1, blocking collectives, per_device(): arrived = lax.all_to_all(blocks, 'lev', 0, 0, tiled=True)  17.8 us
    all_to_all x1, blocking collectives, per_device(): ends = lax.all_to_all(ends, 'lev', 0, 0, tiled=True)  11.9 us
    ppermute x1, starting transfers between devices, per_device(): lax.ppermute(second_own, 'tile', [(i, (i + 1 if i % 2 else i - 1) % TILES...  10.9 us
    ppermute x1, starting transfers between devices, per_device(): first = lax.ppermute(near, 'tile', [(i, i ^ 1) for i in range(TILES)])  2.92 us
    pallas_call x1, Pallas kernels, pack(): call(pack_body, outs, specs, scratch, out_spec=(HBM,) + (VMEM,) * 5)  1.9 us
    pallas_call x1, Pallas kernels, per_device(): call(force_body, ((ROWS, LON, LAT),), [VMEM] * 2, limit=24 << 20, moved=2...  1.49 us
  transfers between devices with their start and end apart: 3, of which 1 were waited for; matrix products, arithmetic and copies ran while one was open for 0% of the time, Pallas kernels for 2%

profile of v6, /device:TPU:1, one launch (start us, length us, event | category | flops | bytes accessed | tf_op | source)
XLA Modules:
  0.0 68.2 jit_solution(5556925346547726624)
XLA Ops:
  0.0 1.9 %shard_map.73 = (f32[320,128]{1,0:T(8,128)}, f32[20,256]{1,0:T(8,128)S(1)}, f32[20,256]{1,0:T(8,128)S(1)}, f32[16,32,256]{2,1,0:T(8,128)S(1)}, f32[3,3,32,256]{3,2,1,0:T(8,128)S(1)}, /*index=5*/f32[3,32,256]{2,1,0:T(8,128)S(1)}) custom-call(s32[1]{0:T(128)} %bitcast.tile.place, s32[1]{0:T(128)} %bitcast.1.place, f32[512,64]{1,0:T(8,128)} %bitcast.16, ...), custom_call_target="tpu_custom_call" | custom-call | bytes 1048576 | tf_op jit(solution)/shard_map/pallas_call | solution.py:94
  1.9 19.6 %all-to-all-start = ((f32[64,1,640]{2,1,0:T(1,128)}), f32[64,1,640]{2,1,0:T(1,128)S(1)}, u32[]{:S(2)}, u32[]{:S(2)}) async-start(f32[64,1,640]{2,1,0:T(1,128)} %bitcast.8), calls=%async_computation | async-start | bytes 327680 | tf_op jit(solution)/shard_map/all_to_all | solution.py:257
  21.5 2.9 %collective-permute-start = (f32[20,256]{1,0:T(8,128)S(1)}, f32[20,256]{1,0:T(8,128)S(1)}, u32[]{:S(2)}, u32[]{:S(2)}) collective-permute-start(f32[20,256]{1,0:T(8,128)S(1)} %shard_map.75), channel_id=1, source_target_pairs={{0,8},{8,0},{16,24},{24,16},{32,40},{40,32},{48,56},{56,48},{64,72... | collective-permute-start | bytes 61448 | tf_op jit(solution)/shard_map/ppermute | solution.py:256
  24.4 10.9 %collective-permute-start.1 = (f32[20,256]{1,0:T(8,128)S(1)}, f32[20,256]{1,0:T(8,128)S(1)}, u32[]{:S(2)}, u32[]{:S(2)}) collective-permute-start(f32[20,256]{1,0:T(8,128)S(1)} %get-tuple-element.16.second_own), channel_id=1, source_target_pairs={{0,504},{8,16},{16,8},{24,32},{32,24},{40,48},{48,40},{56,64},{64,... | collective-permute-start | bytes 61448 | tf_op jit(solution)/shard_map/ppermute | solution.py:254
  35.4 0.0 all-to-all-done
  35.4 1.5 %shard_map.74.forced = f32[16,32,256]{2,1,0:T(8,128)S(1)} custom-call(f32[320,128]{1,0:T(8,128)S(1)} %bitcast.14, f32[16,32,256]{2,1,0:T(8,128)S(1)} %get-tuple-element.14.advected), custom_call_target="tpu_custom_call" | custom-call | bytes 2097152 | tf_op jit(solution)/shard_map/pallas_call | solution.py:258
  36.9 0.0 collective-permute-done.first
  36.9 0.6 collective-permute-done.1.second
  37.4 0.1 shard_map.76
  37.5 17.8 %all_to_all.15.blocks = f32[8,11,8,128]{3,2,1,0:T(8,128)S(1)} all-to-all(f32[8,11,8,128]{3,2,1,0:T(8,128)S(1)} %get-tuple-element.20), channel_id=1, replica_groups=mesh['tile'=64,'lev'=8] {'lev'}, dimensions={0} | all-to-all | bytes 720896 | tf_op jit(solution)/shard_map/all_to_all | solution.py:262
  55.3 0.1 shard_map.77
  55.4 11.9 %all_to_all.16.ends = f32[8,8,8,128]{3,2,1,0:T(8,128)S(1)} all-to-all(f32[8,8,8,128]{3,2,1,0:T(8,128)S(1)} %shard_map.77), channel_id=1, replica_groups=mesh['tile'=64,'lev'=8] {'lev'}, dimensions={0} | all-to-all | bytes 524288 | tf_op jit(solution)/shard_map/all_to_all | solution.py:264
  67.3 0.8 %shard_map.78 = f32[16,32,256]{2,1,0:T(8,128)} custom-call(f32[4,3,32,256]{3,2,1,0:T(8,128)S(1)} %get-tuple-element.19.inner, f32[8,8,8,128]{3,2,1,0:T(8,128)S(1)} %all_to_all.16.ends, f32[3,3,32,256]{3,2,1,0:T(8,128)S(1)} %get-tuple-element.17.carry), custom_call_target="tpu_custom_call" | custom-call | bytes 1048576 | tf_op jit(solution)/shard_map/pallas_call | solution.py:266
  (1 shorter events, 0.0 us)
Async XLA Ops:
  1.9 33.5 %all-to-all-start = ((f32[64,1,640]{2,1,0:T(1,128)}), f32[64,1,640]{2,1,0:T(1,128)S(1)}, u32[]{:S(2)}, u32[]{:S(2)}) async-start(f32[64,1,640]{2,1,0:T(1,128)} %bitcast.8), calls=%async_computation | async-start | bytes 327680 | tf_op jit(solution)/shard_map/all_to_all | solution.py:257
  21.5 15.4 %collective-permute-start = (f32[20,256]{1,0:T(8,128)S(1)}, f32[20,256]{1,0:T(8,128)S(1)}, u32[]{:S(2)}, u32[]{:S(2)}) collective-permute-start(f32[20,256]{1,0:T(8,128)S(1)} %shard_map.75), channel_id=1, source_target_pairs={{0,8},{8,0},{16,24},{24,16},{32,40},{40,32},{48,56},{56,48},{64,72... | collective-permute-start | bytes 61448 | tf_op jit(solution)/shard_map/ppermute | solution.py:256
  24.4 13.0 %collective-permute-start.1 = (f32[20,256]{1,0:T(8,128)S(1)}, f32[20,256]{1,0:T(8,128)S(1)}, u32[]{:S(2)}, u32[]{:S(2)}) collective-permute-start(f32[20,256]{1,0:T(8,128)S(1)} %get-tuple-element.16.second_own), channel_id=1, source_target_pairs={{0,504},{8,16},{16,8},{24,32},{32,24},{40,48},{48,40},{56,64},{64,... | collective-permute-start | bytes 61448 | tf_op jit(solution)/shard_map/ppermute | solution.py:254

commit v7 on v5

--- a/solution.py
+++ b/solution.py
@@ -231,9 +231,10 @@
             level = inner[tracer, lev - 1] + carry[0, lev - 1] * bottom + carry[1, lev - 1] * level
             result[tracer * LEV_DEV + lev] = level
         result[tracer * LEV_DEV] = bottom
-        mine = pl.ds(tracer * LEV_DEV, LEV_DEV)
-        copies.append(pltpu.make_async_copy(result.at[mine], out.at[mine], sems.at[tracer]))
-        copies[-1].start()
+        if tracer % 2 == 1:
+            mine = pl.ds((tracer - 1) * LEV_DEV, 2 * LEV_DEV)
+            copies.append(pltpu.make_async_copy(result.at[mine], out.at[mine], sems.at[tracer // 2]))
+            copies[-1].start()
     for copy in copies:
         copy.wait()
 
@@ -257,7 +258,7 @@
     arrived = lax.all_to_all(blocks, "lev", 0, 0, tiled=True)
     (ends,) = call(chain_body, ((LEVS, 2 * TRACERS, 8, 128),), [VMEM])(arrived)
     ends = lax.all_to_all(ends, "lev", 0, 0, tiled=True)
-    scratch = [pltpu.VMEM((ROWS, LON, LAT), F32), pltpu.SemaphoreType.DMA((TRACERS,))]
+    scratch = [pltpu.VMEM((ROWS, LON, LAT), F32), pltpu.SemaphoreType.DMA((TRACERS // 2,))]
     (updated,) = call(solve_body, ((ROWS, LON, LAT),), [VMEM] * 3, scratch, out_spec=HBM)(inner, ends, carry)
     return updated.reshape(adjoint.shape)
 

time: 68.5 us -> 68.5 us (level)
  no operation moved by 1% of the time
where the time goes in v7:
time: 68.5 us; the launch traced here: 68.2 us
  starting transfers between devices  33.4 us (49%)
  blocking collectives  29.7 us (43%)
  Pallas kernels  4.44 us (6%)
    all_to_all x1, starting transfers between devices, per_device(): lax.all_to_all(payload.reshape(TILES, 1, 640), 'tile', 0, 0, tiled=True)  19.6 us
    all_to_all x1, blocking collectives, per_device(): arrived = lax.all_to_all(blocks, 'lev', 0, 0, tiled=True)  17.8 us
    all_to_all x1, blocking collectives, per_device(): ends = lax.all_to_all(ends, 'lev', 0, 0, tiled=True)  11.9 us
    ppermute x1, starting transfers between devices, per_device(): lax.ppermute(second_own, 'tile', [(i, (i + 1 if i % 2 else i - 1) % TILES...  10.9 us
    ppermute x1, starting transfers between devices, per_device(): first = lax.ppermute(first_own, 'tile', [(i, i ^ 1) for i in range(TILES)])  2.92 us
    pallas_call x1, Pallas kernels, pack(): call(pack_body, outs, specs, scratch, out_spec=(HBM,) + (VMEM,) * 5)  1.9 us
    pallas_call x1, Pallas kernels, per_device(): call(force_body, ((ROWS, LON, LAT),), [VMEM] * 2, limit=24 << 20, moved=2...  1.49 us
  transfers between devices with their start and end apart: 3, of which 1 were waited for; matrix products, arithmetic and copies ran while one was open for 0% of the time, Pallas kernels for 2%

profile of v7, /device:TPU:1, one launch (start us, length us, event | category | flops | bytes accessed | tf_op | source)
XLA Modules:
  0.0 68.2 jit_solution(7103952774341909432)
XLA Ops:
  0.0 1.9 %shard_map.73 = (f32[320,128]{1,0:T(8,128)}, f32[20,256]{1,0:T(8,128)S(1)}, f32[20,256]{1,0:T(8,128)S(1)}, f32[16,32,256]{2,1,0:T(8,128)S(1)}, f32[3,3,32,256]{3,2,1,0:T(8,128)S(1)}, /*index=5*/f32[3,32,256]{2,1,0:T(8,128)S(1)}) custom-call(s32[1]{0:T(128)} %bitcast.tile.place, s32[1]{0:T(128)} %bitcast.1.place, f32[512,64]{1,0:T(8,128)} %bitcast.16, ...), custom_call_target="tpu_custom_call" | custom-call | bytes 1048576 | tf_op jit(solution)/shard_map/pallas_call | solution.py:94
  1.9 19.6 %all-to-all-start = ((f32[64,1,640]{2,1,0:T(1,128)}), f32[64,1,640]{2,1,0:T(1,128)S(1)}, u32[]{:S(2)}, u32[]{:S(2)}) async-start(f32[64,1,640]{2,1,0:T(1,128)} %bitcast.8), calls=%async_computation | async-start | bytes 327680 | tf_op jit(solution)/shard_map/all_to_all | solution.py:253
  21.5 2.9 %collective-permute-start = (f32[20,256]{1,0:T(8,128)S(1)}, f32[20,256]{1,0:T(8,128)S(1)}, u32[]{:S(2)}, u32[]{:S(2)}) collective-permute-start(f32[20,256]{1,0:T(8,128)S(1)} %get-tuple-element.15.first_own), channel_id=1, source_target_pairs={{0,8},{8,0},{16,24},{24,16},{32,40},{40,32},{48,56},{56,48},{64,72... | collective-permute-start | bytes 61448 | tf_op jit(solution)/shard_map/ppermute | solution.py:252
  24.4 10.9 %collective-permute-start.1 = (f32[20,256]{1,0:T(8,128)S(1)}, f32[20,256]{1,0:T(8,128)S(1)}, u32[]{:S(2)}, u32[]{:S(2)}) collective-permute-start(f32[20,256]{1,0:T(8,128)S(1)} %get-tuple-element.16.second_own), channel_id=1, source_target_pairs={{0,504},{8,16},{16,8},{24,32},{32,24},{40,48},{48,40},{56,64},{64,... | collective-permute-start | bytes 61448 | tf_op jit(solution)/shard_map/ppermute | solution.py:251
  35.3 0.0 all-to-all-done
  35.4 1.5 %shard_map.74.forced = f32[16,32,256]{2,1,0:T(8,128)S(1)} custom-call(f32[320,128]{1,0:T(8,128)S(1)} %bitcast.14, f32[16,32,256]{2,1,0:T(8,128)S(1)} %get-tuple-element.14.advected), custom_call_target="tpu_custom_call" | custom-call | bytes 2097152 | tf_op jit(solution)/shard_map/pallas_call | solution.py:254
  36.9 0.0 collective-permute-done.first
  36.9 0.6 collective-permute-done.1.second
  37.4 0.1 shard_map.75
  37.5 17.8 %all_to_all.15.blocks = f32[8,11,8,128]{3,2,1,0:T(8,128)S(1)} all-to-all(f32[8,11,8,128]{3,2,1,0:T(8,128)S(1)} %get-tuple-element.20), channel_id=1, replica_groups=mesh['tile'=64,'lev'=8] {'lev'}, dimensions={0} | all-to-all | bytes 720896 | tf_op jit(solution)/shard_map/all_to_all | solution.py:258
  55.3 0.1 shard_map.76
  55.4 11.9 %all_to_all.16.ends = f32[8,8,8,128]{3,2,1,0:T(8,128)S(1)} all-to-all(f32[8,8,8,128]{3,2,1,0:T(8,128)S(1)} %shard_map.76), channel_id=1, replica_groups=mesh['tile'=64,'lev'=8] {'lev'}, dimensions={0} | all-to-all | bytes 524288 | tf_op jit(solution)/shard_map/all_to_all | solution.py:260
  67.3 0.9 %shard_map.77 = f32[16,32,256]{2,1,0:T(8,128)} custom-call(f32[4,3,32,256]{3,2,1,0:T(8,128)S(1)} %get-tuple-element.19.inner, f32[8,8,8,128]{3,2,1,0:T(8,128)S(1)} %all_to_all.16.ends, f32[3,3,32,256]{3,2,1,0:T(8,128)S(1)} %get-tuple-element.17.carry), custom_call_target="tpu_custom_call" | custom-call | bytes 1048576 | tf_op jit(solution)/shard_map/pallas_call | solution.py:262
Async XLA Ops:
  1.9 33.4 %all-to-all-start = ((f32[64,1,640]{2,1,0:T(1,128)}), f32[64,1,640]{2,1,0:T(1,128)S(1)}, u32[]{:S(2)}, u32[]{:S(2)}) async-start(f32[64,1,640]{2,1,0:T(1,128)} %bitcast.8), calls=%async_computation | async-start | bytes 327680 | tf_op jit(solution)/shard_map/all_to_all | solution.py:253
  21.5 15.4 %collective-permute-start = (f32[20,256]{1,0:T(8,128)S(1)}, f32[20,256]{1,0:T(8,128)S(1)}, u32[]{:S(2)}, u32[]{:S(2)}) collective-permute-start(f32[20,256]{1,0:T(8,128)S(1)} %get-tuple-element.15.first_own), channel_id=1, source_target_pairs={{0,8},{8,0},{16,24},{24,16},{32,40},{40,32},{48,56},{56,48},{64,72... | collective-permute-start | bytes 61448 | tf_op jit(solution)/shard_map/ppermute | solution.py:252
  24.4 13.0 %collective-permute-start.1 = (f32[20,256]{1,0:T(8,128)S(1)}, f32[20,256]{1,0:T(8,128)S(1)}, u32[]{:S(2)}, u32[]{:S(2)}) collective-permute-start(f32[20,256]{1,0:T(8,128)S(1)} %get-tuple-element.16.second_own), channel_id=1, source_target_pairs={{0,504},{8,16},{16,8},{24,32},{32,24},{40,48},{48,40},{56,64},{64,... | collective-permute-start | bytes 61448 | tf_op jit(solution)/shard_map/ppermute | solution.py:251
